TPU v7x, 32 devices: a whole 2x2x4 slice. The times are simulated.
32 devices in a mesh: modes: 4 (over y, core), sites: 8 (over z, x).
Axes of the slice: x: 2, y: 2, z: 4, core: 2. Of those that a mesh axis runs over, the one named last changes fastest.
Arguments:
- eigvecs: bfloat16 [2, 2048, 12, 4096], P(None, 'modes', None, 'sites'), may hold values from -6 to 6
- eigenvalues: float32 [2048], P('modes'), may hold values from -64 to 64, as said below
- source_sites: int32 [2], replicated, may hold values from 0 to 4095
Outputs:
- propagator: float32 [24, 2, 12, 4096], P('modes', None, None, 'sites')
Inputs may be any that keep to these rules, and one draw needn't show every extreme that they name: `eigenvalues`: magnitudes between 8 and 64, of either sign.
All inputs are finite; a program needn't handle non-finite values.
Results may differ from a plain program's by a relative error of at most 0.0029.
Values may be sent and summed in bfloat16 or wider, within the bound.
No kernel may reach another device: no remote copies, remote signals or barrier semaphores. Data moves between devices by JAX's collectives and lax.ppermute only.
A program may use at most 128 MiB of HBM per device.

v0:
```python
import jax
import jax.numpy as jnp
from jax import lax
from jax.sharding import PartitionSpec as P


def spread(block, axis, owner):
    block = jnp.where(lax.axis_index(axis) == owner, block, jnp.zeros_like(block))
    return lax.psum(block, axis)


def weight_table(source_rows, eigenvalues):
    divisor = eigenvalues[:, None]
    weight_real = (source_rows[0].astype(jnp.float32) / divisor).astype(jnp.bfloat16)
    weight_imag = (-source_rows[1].astype(jnp.float32) / divisor).astype(jnp.bfloat16)
    column_real = jnp.concatenate([weight_real, -weight_imag], axis=0)
    column_imag = jnp.concatenate([weight_imag, weight_real], axis=0)
    return jnp.stack([column_real, column_imag], axis=2)


def project(weights, flattened):
    return jnp.dot(weights.T, flattened, preferred_element_type=jnp.float32)


def on_device(eigvecs, eigenvalues, source_sites):
    mode_count = eigvecs.shape[1]
    spin_color = eigvecs.shape[2]
    site_count = eigvecs.shape[3]
    source_count = source_sites.shape[0]
    offset = lax.axis_index("sites") * site_count
    local_index = jnp.clip(source_sites - offset, 0, site_count - 1)
    picked = [
        lax.dynamic_slice_in_dim(eigvecs, local_index[number], 1, 3)
        for number in range(source_count)
    ]

    def fetch_row(piece, owner):
        return spread(piece, "sites", owner)

    received = [
        fetch_row(picked[number], source_sites[number] // site_count)
        for number in range(source_count)
    ]
    gathered = jnp.concatenate(received, axis=3)
    columns = source_count * spin_color
    source_rows = jnp.transpose(gathered, (0, 1, 3, 2)).reshape(2, mode_count, columns)
    col_share = columns // lax.axis_size("modes")
    flattened = eigvecs.reshape(2 * mode_count, spin_color * site_count)
    weights = weight_table(source_rows, eigenvalues).reshape(2 * mode_count, 2 * columns)
    partial_value = project(weights, flattened).reshape(columns, 2, spin_color, site_count)
    summed = lax.psum(partial_value, "modes")
    return lax.dynamic_slice_in_dim(summed, lax.axis_index("modes") * col_share, col_share, 0)


def solution(mesh):
    in_specs = (P(None, "modes", None, "sites"), P("modes"), P())
    out_specs = P("modes", None, None, "sites")
    return jax.shard_map(
        on_device, mesh=mesh, in_specs=in_specs, out_specs=out_specs, check_vma=False
    )
```

profile of v0, /device:TPU:0, one launch (start us, length us, event | category | flops | bytes accessed | tf_op | source)
XLA Modules:
  0.0 166.4 jit_solution(7186072740592180763)
XLA Ops:
  6.5 0.0 all-reduce.3.cloned.1.call-start
  6.5 0.7 subtract_clamp_fusion
  7.2 0.6 fusion.4
  10.1 1.4 fusion.3
  16.5 31.4 %copy.14 = bf16[2,512,12,512]{1,0,3,2:T(2,128)(2,1)} copy(bf16[2,512,12,512]{3,1,2,0:T(8,128)(2,1)} %param.3) | data formatting | bytes 25165824 | tf_op args[0]
  49.1 6.5 %constant_dynamic-slice_fusion.2 = (bf16[2,512,12,1]{3,1,2,0:T(8,128)(2,1)S(1)}, bf16[2,512,12,1]{3,1,2,0:T(8,128)(2,1)}) fusion(bf16[2,512,12,512]{3,1,2,0:T(8,128)(2,1)} %param.3, s32[]{:T(128)S(6)} %select_n.33, s32[]{:T(128)S(6)} %select_n.37), kind=kLoop, calls=%fused_computation.14 | loop fusion | bytes 98312 | tf_op jit(solution)/shard_map/dynamic_slice | solution.py:33
  55.6 3.5 %copy.21 = bf16[2,512,12,1]{1,2,3,0:T(8,128)(2,1)S(1)} copy(bf16[2,512,12,1]{3,1,2,0:T(8,128)(2,1)} %get-tuple-element.10) | data formatting | bytes 49152
  59.1 1.7 %copy.20 = bf16[2,512,12,1]{1,2,3,0:T(8,128)(2,1)S(1)} copy(bf16[2,512,12,1]{3,1,2,0:T(8,128)(2,1)S(1)} %get-tuple-element.9) | data formatting | bytes 49152
  60.9 39.3 %all-reduce = (bf16[2,512,12,1]{1,2,3,0:T(8,128)(2,1)S(1)}, bf16[2,512,12,1]{1,2,3,0:T(8,128)(2,1)S(1)}) all-reduce(bf16[2,512,12,1]{1,2,3,0:T(8,128)(2,1)S(1)} %get-tuple-element.17, bf16[2,512,12,1]{1,2,3,0:T(8,128)(2,1)S(1)} %get-tuple-element.18), channel_id=1, replica_groups=mesh['modes'=4,'sites'=8] {'sites'}, use_global_device_ids=true, to_apply=%region_1.2 | all-reduce | flops 24576 | bytes 98304 | tf_op jit(solution)/shard_map/psum | solution.py:9
  100.2 0.0 copy-start
  100.2 12.7 %copy.22 = bf16[768,8,2,512]{3,1,2,0:T(8,128)(2,1)} copy(bf16[768,8,2,512]{3,2,1,0:T(2,128)(2,1)} %bitcast.30) | data formatting | bytes 25165824
  112.9 0.0 copy-done
  113.0 0.1 copy.13
  113.2 9.5 %fusion = f32[24,2,12,512]{3,0,2,1:T(8,128)} fusion(bf16[12,512,1024,1]{2,1,0,3:T(8,128)(2,1)} %bitcast.31, bf16[24,2,1024,1]{2,1,0,3:T(2,128)(2,1)S(1)} %bitcast.32), kind=kOutput, calls=%fused_computation.1 | convolution fusion | flops 603979776 | bytes 13860864 | tf_op jit(solution)/shard_map/dot_general | solution.py:22
  122.7 0.0 all-reduce.3.cloned.1.call-update
  122.7 34.7 %all-reduce.3.cloned.1.call-done = f32[24,2,12,512]{3,0,2,1:T(8,128)} async-done(((f32[24,2,12,512]{3,0,2,1:T(8,128)}), f32[24,2,12,512]{3,0,2,1:T(8,128)}) %all-reduce.3.cloned.1.call-update) | async-done | bytes 1179664 | tf_op jit(solution)/shard_map/psum | solution.py:51
  157.4 1.2 constant_dynamic-slice_fusion
  158.6 0.9 copy.16
  (12 shorter events, 0.2 us)
Async XLA Ops:
  6.5 150.9 %all-reduce.3.cloned.1.call-start = ((), (), s32[]{:S(2)}) async-start(), calls=%async_computation | async-start | bytes 2359296 | tf_op jit(solution)/shard_map/psum | solution.py:51
  100.2 12.7 %copy-start = (f32[512]{0:T(512)S(1)}, f32[512]{0:T(512)}, u32[]{:S(2)}) copy-start(f32[512]{0:T(512)} %param.4) | copy-start | bytes 6148
Sparse Core Ops, SparseCore 0:
  122.8 34.5 all-reduce.2
where the time goes:
time: 168 us; the launch traced here: 166 us
  local copies, waits for them, and re-layouts  60 us (36%)
  blocking collectives  39.3 us (23%)
  waiting for transfers between devices  34.7 us (21%)
  between operations  22.2 us (13%)
  matrix products  9.46 us (6%)
    unnamed x6, local copies, waits for them, and re-layouts  49.3 us
    psum x1, blocking collectives, spread(): return lax.psum(block, axis)  39.3 us
    psum x1, waiting for transfers between devices, on_device(): summed = lax.psum(partial_value, 'modes')  34.7 us
    dot_general x1, matrix products, project(): return jnp.dot(weights.T, flattened, preferred_element_type=jnp.float32)  9.46 us
    dynamic_slice x1, local copies, waits for them, and re-layouts, on_device(): lax.dynamic_slice_in_dim(eigvecs, local_index[number], 1, 3)  6.48 us
  transfers between devices with their start and end apart: 1, of which 1 were waited for; matrix products, arithmetic and copies ran while one was open for 0% of the time, Pallas kernels for 0%

commit v1 on v0

v1 whole, which is shorter than its diff:
```python
import functools
import jax
import jax.numpy as jnp
from jax import lax
from jax.experimental import pallas as pl
from jax.experimental.pallas import tpu as pltpu
from jax.sharding import PartitionSpec as P

LANES = 128
MIB = 2**20


def pick_kernel(sites_ref, vectors_ref, rows_ref, columns_ref, total_ref, sems):
    parts, spin_color, mode_count, site_count = vectors_ref.shape
    source_count = sites_ref.shape[0]
    columns = source_count * spin_color
    first = lax.axis_index("sites") * site_count
    local = [sites_ref[number] - first for number in range(source_count)]
    held = [(index >= 0) & (index < site_count) for index in local]

    def copy(number, part):
        start = pl.multiple_of(local[number] // LANES * LANES, LANES)
        return pltpu.make_async_copy(
            vectors_ref.at[part, :, :, pl.ds(start, LANES)],
            columns_ref.at[number, part],
            sems.at[number, part],
        )

    for number in range(source_count):
        @pl.when(held[number])
        def _(number=number):
            for part in range(parts):
                copy(number, part).start()

    total_ref[...] = jnp.zeros_like(total_ref)
    row = lax.broadcasted_iota(jnp.int32, (columns, LANES), 0)
    lane = lax.broadcasted_iota(jnp.int32, (columns, LANES), 1)
    for number in range(source_count):
        @pl.when(held[number])
        def _(number=number):
            for part in range(parts):
                copy(number, part).wait()
                total = jnp.zeros((columns, mode_count), jnp.float32)
                for component in range(spin_color):
                    chosen = (row == number * spin_color + component) & (lane == local[number] % LANES)
                    total += lax.dot_general(
                        jnp.where(chosen, 1.0, 0.0).astype(jnp.bfloat16),
                        columns_ref[number, part, component],
                        (((1,), (1,)), ((), ())),
                        preferred_element_type=jnp.float32,
                    )
                total_ref[pl.ds(part * columns, columns), :] += total
    rows_ref[...] = total_ref[...].astype(rows_ref.dtype)


def pick(source_sites, vectors):
    parts, spin_color, mode_count, site_count = vectors.shape
    source_count = source_sites.shape[0]
    rows = parts * source_count * spin_color
    return pl.pallas_call(
        pick_kernel,
        out_shape=jax.ShapeDtypeStruct((rows, mode_count), vectors.dtype),
        in_specs=[pl.BlockSpec(memory_space=pltpu.SMEM), pl.BlockSpec(memory_space=pl.ANY)],
        out_specs=pl.BlockSpec(memory_space=pltpu.VMEM),
        scratch_shapes=[
            pltpu.VMEM((source_count, parts, spin_color, mode_count, LANES), vectors.dtype),
            pltpu.VMEM((rows, mode_count), jnp.float32),
            pltpu.SemaphoreType.DMA((source_count, parts)),
        ],
        compiler_params=pltpu.CompilerParams(vmem_limit_bytes=16 * MIB),
        name="pick",
    )(source_sites, vectors)


def iota(shape, dim):
    return lax.broadcasted_iota(jnp.int32, shape, dim)


def shares(columns, ways, core, plane):
    share = columns // ways
    shape = (2 * columns, 2 * columns)
    row, entry = iota(shape, 0), iota(shape, 1)
    place, inner = row // (2 * share), row % (2 * share)
    its_core = jnp.where(place < 2, 1 - core, core)
    its_plane = jnp.where((place == 0) | (place == 3), plane, 1 - plane)
    column, part = (2 * its_plane + its_core) * share + inner // 2, inner % 2
    real, imag = (entry == column), (entry == column + columns)
    one = jnp.float32(1)
    zero = jnp.float32(0)
    on_real = jnp.where(part == 0, jnp.where(real, one, zero), jnp.where(imag, one, zero))
    on_imag = jnp.where(part == 0, jnp.where(imag, -one, zero), jnp.where(real, one, zero))
    return on_real.astype(jnp.bfloat16), on_imag.astype(jnp.bfloat16)


def dot(left, right):
    return jnp.dot(left, right, preferred_element_type=jnp.float32)


def project_kernel(rows_ref, values_ref, vectors_ref, sent_ref, kept_ref, flat_ref):
    parts, spin_color, mode_count, site_count = vectors_ref.shape
    columns = rows_ref.shape[0] // 2
    ways = 4
    share = 2 * columns // ways
    index = lax.axis_index("modes")
    divisor = values_ref[...]
    real = rows_ref[:columns, :].astype(jnp.float32) / divisor
    imag = -rows_ref[columns:, :].astype(jnp.float32) / divisor
    weights = jnp.concatenate([real, imag], axis=0).astype(jnp.bfloat16)
    on_real, on_imag = shares(columns, ways, index % 2, index // 2)
    left_real = dot(on_real, weights).astype(jnp.bfloat16)
    left_imag = dot(on_imag, weights).astype(jnp.bfloat16)
    for component in range(spin_color):
        product = dot(left_real, vectors_ref[0, component]) + dot(left_imag, vectors_ref[1, component])
        for place in range(ways):
            flat_ref[place, pl.ds(component * share, share), :] = product[place * share:(place + 1) * share]
    sent_ref[...] = flat_ref[:2].astype(sent_ref.dtype)
    kept_ref[...] = flat_ref[2:].astype(kept_ref.dtype)


def project(rows, eigenvalues, vectors):
    parts, spin_color, mode_count, site_count = vectors.shape
    share = rows.shape[0] // 4 * spin_color
    shape = (2, share, site_count)
    return pl.pallas_call(
        project_kernel,
        out_shape=[jax.ShapeDtypeStruct(shape, jnp.bfloat16), jax.ShapeDtypeStruct(shape, jnp.float32)],
        in_specs=[pl.BlockSpec(memory_space=pltpu.VMEM)] * 3,
        out_specs=[pl.BlockSpec(memory_space=pltpu.VMEM)] * 2,
        scratch_shapes=[pltpu.VMEM((4, share, site_count), jnp.float32)],
        compiler_params=pltpu.CompilerParams(vmem_limit_bytes=32 * MIB),
        name="project",
    )(rows, eigenvalues.reshape(1, mode_count), vectors)


def swap(block, axis, size, bit):
    return lax.ppermute(block, axis, [(index, index ^ bit) for index in range(size)])


def on_device(eigvecs, eigenvalues, source_sites):
    site_ways, mode_ways = lax.axis_size("sites"), lax.axis_size("modes")
    vectors = jnp.transpose(eigvecs, (0, 2, 1, 3))
    parts, spin_color, mode_count, site_count = vectors.shape
    rows = pick(source_sites, vectors)
    bit = 1
    while bit < site_ways:
        rows = rows + swap(rows, "sites", site_ways, bit)
        bit *= 2
    sent, kept = project(rows, eigenvalues, vectors)
    got = swap(sent, "modes", mode_ways, 1)
    across = (kept[0] + got[1].astype(jnp.float32)).astype(jnp.bfloat16)
    arrived = swap(across, "modes", mode_ways, 2)
    total = kept[1] + got[0].astype(jnp.float32) + arrived.astype(jnp.float32)
    share = total.shape[0] // spin_color // 2
    return jnp.transpose(total.reshape(spin_color, share, 2, site_count), (1, 2, 0, 3))


def solution(mesh):
    in_specs = (P(None, "modes", None, "sites"), P("modes"), P())
    out_specs = P("modes", None, None, "sites")
    return jax.shard_map(on_device, mesh=mesh, in_specs=in_specs, out_specs=out_specs, check_vma=False)
```

time: 168 us -> 33.4 us (0.20)
  local copies, waits for them, and re-layouts: 60 us -> 6.14 us
  blocking collectives: 39.3 us -> 0 us
  between operations: 22.2 us -> 0.08 us
  waiting for transfers between devices: 34.7 us -> 14.1 us
  matrix products: 9.46 us -> 0 us
  starting transfers between devices: 0.01 us -> 8.05 us
  Pallas kernels: 0 us -> 4.88 us
    unnamed x6 -> x8, local copies, waits for them, and re-layouts: 49.3 us -> 5.24 us
    psum x1 -> x0, blocking collectives: 39.3 us -> none  [spread(): return lax.psum(block, axis)]
    psum x1 -> x0, waiting for transfers between devices: 34.7 us -> none  [on_device(): summed = lax.psum(partial_value, 'modes')]
    ppermute x0 -> x5, waiting for transfers between devices: none -> 14.1 us  [swap(): lax.ppermute(block, axis, [(index, index ^ bit) for index in range(size)])]
    dot_general x1 -> x0, matrix products: 9.46 us -> none  [project(): return jnp.dot(weights.T, flattened, preferred_element_type=jnp.float32)]
    dynamic_slice x3 -> x0, local copies, waits for them, and re-layouts: 8.61 us -> none  [the longest x1 6.48 us: on_device(): lax.dynamic_slice_in_dim(eigvecs, local_index[number], 1, 3)]
    ppermute x0 -> x5, starting transfers between devices: none -> 8.05 us  [swap(): lax.ppermute(block, axis, [(index, index ^ bit) for index in range(size)])]
    pallas_call x0 -> x2, Pallas kernels: none -> 4.88 us  [the longest x1 2.47 us: project(): pl.pallas_call(project_kernel, out_shape=[jax.ShapeDtypeStruct(shape, jnp...]
  transfers between devices with their start and end apart: 1 -> 5, of which waited for: 1 -> 5; matrix products, arithmetic and copies ran while one was open for 0% -> 0% of each run, Pallas kernels for 0% -> 0%
where the time goes in v1:
time: 33.4 us
  waiting for transfers between devices  14.1 us (42%)
  starting transfers between devices  8.05 us (24%)
  local copies, waits for them, and re-layouts  6.14 us (18%)
  Pallas kernels  4.88 us (15%)
    ppermute x5, waiting for transfers between devices, swap(): lax.ppermute(block, axis, [(index, index ^ bit) for index in range(size)])  14.1 us
    ppermute x5, starting transfers between devices, swap(): lax.ppermute(block, axis, [(index, index ^ bit) for index in range(size)])  8.05 us
    unnamed x8, local copies, waits for them, and re-layouts  5.24 us
    pallas_call x1, Pallas kernels, project(): pl.pallas_call(project_kernel, out_shape=[jax.ShapeDtypeStruct(shape, jnp...  2.47 us
    pallas_call x1, Pallas kernels, pick(): pl.pallas_call(pick_kernel, out_shape=jax.ShapeDtypeStruct((rows, mode_co...  2.42 us
    reshape x2, local copies, waits for them, and re-layouts, on_device(): total.reshape(spin_color, share, 2, site_count)  0.9 us
  transfers between devices with their start and end apart: 5, of which 5 were waited for; matrix products, arithmetic and copies ran while one was open for 0% of the time, Pallas kernels for 0%

profile of v1, /device:TPU:0, one launch (start us, length us, event | category | flops | bytes accessed | tf_op | source)
XLA Modules:
  0.0 33.4 jit_solution(2587526056997348818)
XLA Ops:
  0.0 0.0 copy-start
  0.0 4.6 %copy-done = bf16[2,512,12,512]{3,1,2,0:T(8,128)(2,1)S(1)} copy-done((bf16[2,512,12,512]{3,1,2,0:T(8,128)(2,1)S(1)}, bf16[2,512,12,512]{3,1,2,0:T(8,128)(2,1)}, u32[]{:S(2)}) %copy-start) | copy-done | bytes 12582936
  4.6 0.0 copy-start.3
  4.6 0.7 %copy-done.3 = s32[2]{0:T(128)S(1)} copy-done((s32[2]{0:T(128)S(1)}, s32[2]{0:T(128)}, u32[]{:S(2)}) %copy-start.3) | copy-done | bytes 32
  5.2 0.0 copy-start.1
  5.2 0.0 copy-start.2
  5.2 2.4 %pick.1 = bf16[48,512]{1,0:T(8,128)(2,1)S(1)} custom-call(s32[2]{0:T(128)S(1)} %copy-done.3, bf16[2,12,512,512]{3,2,1,0:T(8,128)(2,1)S(1)} %bitcast.9), custom_call_target="tpu_custom_call" | custom-call | tf_op jit(solution)/shard_map/pick/pallas_call | solution.py:60
  7.7 1.2 %collective-permute-start = (bf16[48,512]{1,0:T(8,128)(2,1)S(1)}, bf16[48,512]{1,0:T(8,128)(2,1)S(1)}, u32[]{:S(2)}, u32[]{:S(2)}) collective-permute-start(bf16[48,512]{1,0:T(8,128)(2,1)S(1)} %pick.1), channel_id=1, source_target_pairs={{0,1},{1,0},{2,3},{3,2},{4,5},{5,4},{6,7},{7,6},{8,9},{9,8},{10,11... | collective-permute-start | bytes 147464 | tf_op jit(solution)/shard_map/ppermute | solution.py:136
  8.9 3.0 %collective-permute-done = bf16[48,512]{1,0:T(8,128)(2,1)S(1)} collective-permute-done((bf16[48,512]{1,0:T(8,128)(2,1)S(1)}, bf16[48,512]{1,0:T(8,128)(2,1)S(1)}, u32[]{:S(2)}, u32[]{:S(2)}) %collective-permute-start) | collective-permute-done | bytes 49184 | tf_op jit(solution)/shard_map/ppermute | solution.py:136
  11.8 1.3 %collective-permute-start.1 = (bf16[48,512]{1,0:T(8,128)(2,1)S(1)}, bf16[48,512]{1,0:T(8,128)(2,1)S(1)}, u32[]{:S(2)}, u32[]{:S(2)}) collective-permute-start(bf16[48,512]{1,0:T(8,128)(2,1)S(1)} %add.22), channel_id=1, source_target_pairs={{0,2},{1,3},{2,0},{3,1},{4,6},{5,7},{6,4},{7,5},{8,10},{9,11},{10,... | collective-permute-start | bytes 147464 | tf_op jit(solution)/shard_map/ppermute | solution.py:136
  13.1 2.9 %collective-permute-done.1 = bf16[48,512]{1,0:T(8,128)(2,1)S(1)} collective-permute-done((bf16[48,512]{1,0:T(8,128)(2,1)S(1)}, bf16[48,512]{1,0:T(8,128)(2,1)S(1)}, u32[]{:S(2)}, u32[]{:S(2)}) %collective-permute-start.1) | collective-permute-done | bytes 49184 | tf_op jit(solution)/shard_map/ppermute | solution.py:136
  16.0 3.7 %collective-permute-start.2 = (bf16[48,512]{1,0:T(8,128)(2,1)S(1)}, bf16[48,512]{1,0:T(8,128)(2,1)S(1)}, u32[]{:S(2)}, u32[]{:S(2)}) collective-permute-start(bf16[48,512]{1,0:T(8,128)(2,1)S(1)} %add.23), channel_id=1, source_target_pairs={{0,4},{1,5},{2,6},{3,7},{4,0},{5,1},{6,2},{7,3},{8,12},{9,13},{10,... | collective-permute-start | bytes 147464 | tf_op jit(solution)/shard_map/ppermute | solution.py:136
  19.7 2.6 %collective-permute-done.2 = bf16[48,512]{1,0:T(8,128)(2,1)S(1)} collective-permute-done((bf16[48,512]{1,0:T(8,128)(2,1)S(1)}, bf16[48,512]{1,0:T(8,128)(2,1)S(1)}, u32[]{:S(2)}, u32[]{:S(2)}) %collective-permute-start.2) | collective-permute-done | bytes 49184 | tf_op jit(solution)/shard_map/ppermute | solution.py:136
  22.3 0.0 copy-done.1
  22.3 0.0 copy-done.2
  22.3 2.5 %project.1 = (bf16[2,144,512]{2,1,0:T(8,128)(2,1)S(1)}, f32[2,144,512]{2,1,0:T(8,128)S(1)}) custom-call(bf16[48,512]{1,0:T(8,128)(2,1)S(1)} %add.24.rows_ref, f32[1,512]{1,0:T(1,128)S(1)} %bitcast.11, bf16[2,12,512,512]{3,2,1,0:T(8,128)(2,1)S(1)} %bitcast.10), custom_call_target="tpu_custom_call" | custom-call | tf_op jit(solution)/shard_map/project/pallas_call | solution.py:124
  24.8 0.1 collective-permute-start.3
  24.8 1.6 %collective-permute-done.3 = bf16[2,144,512]{2,1,0:T(8,128)(2,1)S(1)} collective-permute-done((bf16[2,144,512]{2,1,0:T(8,128)(2,1)S(1)}, bf16[2,144,512]{2,1,0:T(8,128)(2,1)S(1)}, u32[]{:S(2)}, u32[]{:S(2)}) %collective-permute-start.3) | collective-permute-done | bytes 294944 | tf_op jit(solution)/shard_map/ppermute | solution.py:136
  26.4 1.9 %collective-permute-start.4 = (bf16[144,512]{1,0:T(8,128)(2,1)S(1)}, bf16[144,512]{1,0:T(8,128)(2,1)S(1)}, u32[]{:S(2)}, u32[]{:S(2)}) collective-permute-start(bf16[144,512]{1,0:T(8,128)(2,1)S(1)} %fusion), channel_id=1, source_target_pairs={{0,16},{8,24},{16,0},{24,8},{1,17},{9,25},{17,1},{25,9},{2,18},{10... | collective-permute-start | bytes 442376 | tf_op jit(solution)/shard_map/ppermute | solution.py:136
  28.3 4.1 %collective-permute-done.4 = bf16[144,512]{1,0:T(8,128)(2,1)S(1)} collective-permute-done((bf16[144,512]{1,0:T(8,128)(2,1)S(1)}, bf16[144,512]{1,0:T(8,128)(2,1)S(1)}, u32[]{:S(2)}, u32[]{:S(2)}) %collective-permute-start.4) | collective-permute-done | bytes 147488 | tf_op jit(solution)/shard_map/ppermute | solution.py:136
  32.5 0.2 reshape.12
  32.7 0.7 %copy.6 = f32[12,6,2,512]{3,2,0,1:T(2,128)} copy(f32[12,6,2,512]{3,2,1,0:T(2,128)S(1)} %reshape.12) | data formatting | bytes 589824 | tf_op jit(solution)/shard_map/reshape | solution.py:154
  (5 shorter events, 0.1 us)
Async XLA Ops:
  0.0 4.6 %copy-start = (bf16[2,512,12,512]{3,1,2,0:T(8,128)(2,1)S(1)}, bf16[2,512,12,512]{3,1,2,0:T(8,128)(2,1)}, u32[]{:S(2)}) copy-start(bf16[2,512,12,512]{3,1,2,0:T(8,128)(2,1)} %param.3) | copy-start | bytes 37748740
  4.6 0.7 %copy-start.3 = (s32[2]{0:T(128)S(1)}, s32[2]{0:T(128)}, u32[]{:S(2)}) copy-start(s32[2]{0:T(128)} %sites_ref.1) | copy-start | bytes 28
  5.2 17.0 %copy-start.1 = (bf16[2,512,12,512]{3,1,2,0:T(8,128)(2,1)S(1)}, bf16[2,512,12,512]{3,1,2,0:T(8,128)(2,1)}, u32[]{:S(2)}) copy-start(bf16[2,512,12,512]{3,1,2,0:T(8,128)(2,1)} %param.3) | copy-start | bytes 37748740
  5.2 17.0 %copy-start.2 = (f32[512]{0:T(512)S(1)}, f32[512]{0:T(512)}, u32[]{:S(2)}) copy-start(f32[512]{0:T(512)} %param.4) | copy-start | bytes 6148
  7.7 4.2 %collective-permute-start = (bf16[48,512]{1,0:T(8,128)(2,1)S(1)}, bf16[48,512]{1,0:T(8,128)(2,1)S(1)}, u32[]{:S(2)}, u32[]{:S(2)}) collective-permute-start(bf16[48,512]{1,0:T(8,128)(2,1)S(1)} %pick.1), channel_id=1, source_target_pairs={{0,1},{1,0},{2,3},{3,2},{4,5},{5,4},{6,7},{7,6},{8,9},{9,8},{10,11... | collective-permute-start | bytes 147464 | tf_op jit(solution)/shard_map/ppermute | solution.py:136
  11.8 4.2 %collective-permute-start.1 = (bf16[48,512]{1,0:T(8,128)(2,1)S(1)}, bf16[48,512]{1,0:T(8,128)(2,1)S(1)}, u32[]{:S(2)}, u32[]{:S(2)}) collective-permute-start(bf16[48,512]{1,0:T(8,128)(2,1)S(1)} %add.22), channel_id=1, source_target_pairs={{0,2},{1,3},{2,0},{3,1},{4,6},{5,7},{6,4},{7,5},{8,10},{9,11},{10,... | collective-permute-start | bytes 147464 | tf_op jit(solution)/shard_map/ppermute | solution.py:136
  16.0 6.2 %collective-permute-start.2 = (bf16[48,512]{1,0:T(8,128)(2,1)S(1)}, bf16[48,512]{1,0:T(8,128)(2,1)S(1)}, u32[]{:S(2)}, u32[]{:S(2)}) collective-permute-start(bf16[48,512]{1,0:T(8,128)(2,1)S(1)} %add.23), channel_id=1, source_target_pairs={{0,4},{1,5},{2,6},{3,7},{4,0},{5,1},{6,2},{7,3},{8,12},{9,13},{10,... | collective-permute-start | bytes 147464 | tf_op jit(solution)/shard_map/ppermute | solution.py:136
  24.8 1.6 %collective-permute-start.3 = (bf16[2,144,512]{2,1,0:T(8,128)(2,1)S(1)}, bf16[2,144,512]{2,1,0:T(8,128)(2,1)S(1)}, u32[]{:S(2)}, u32[]{:S(2)}) collective-permute-start(bf16[2,144,512]{2,1,0:T(8,128)(2,1)S(1)} %get-tuple-element.8), channel_id=1, source_target_pairs={{0,8},{8,0},{16,24},{24,16},{1,9},{9,1},{17,25},{25,17},{2,10},{10... | collective-permute-start | bytes 884744 | tf_op jit(solution)/shard_map/ppermute | solution.py:136
  26.4 6.0 %collective-permute-start.4 = (bf16[144,512]{1,0:T(8,128)(2,1)S(1)}, bf16[144,512]{1,0:T(8,128)(2,1)S(1)}, u32[]{:S(2)}, u32[]{:S(2)}) collective-permute-start(bf16[144,512]{1,0:T(8,128)(2,1)S(1)} %fusion), channel_id=1, source_target_pairs={{0,16},{8,24},{16,0},{24,8},{1,17},{9,25},{17,1},{25,9},{2,18},{10... | collective-permute-start | bytes 442376 | tf_op jit(solution)/shard_map/ppermute | solution.py:136

commit v2 on v1

--- a/solution.py
+++ b/solution.py
@@ -1,4 +1,3 @@
-import functools
 import jax
 import jax.numpy as jnp
 from jax import lax
@@ -8,12 +7,16 @@
 
 LANES = 128
 MIB = 2**20
-
-
-def pick_kernel(sites_ref, vectors_ref, rows_ref, columns_ref, total_ref, sems):
+GROUPS = [[1, 2, 3], [4]]
+
+
+def pick_kernel(given_ref, vectors_ref, rows_ref, sites_ref, columns_ref, total_ref, given_sem, sems):
+    given = pltpu.make_async_copy(given_ref, sites_ref, given_sem)
+    given.start()
+    total_ref[...] = jnp.zeros_like(total_ref)
+    given.wait()
     parts, spin_color, mode_count, site_count = vectors_ref.shape
     source_count = sites_ref.shape[0]
-    columns = source_count * spin_color
     first = lax.axis_index("sites") * site_count
     local = [sites_ref[number] - first for number in range(source_count)]
     held = [(index >= 0) & (index < site_count) for index in local]
@@ -32,24 +35,22 @@
             for part in range(parts):
                 copy(number, part).start()
 
-    total_ref[...] = jnp.zeros_like(total_ref)
-    row = lax.broadcasted_iota(jnp.int32, (columns, LANES), 0)
-    lane = lax.broadcasted_iota(jnp.int32, (columns, LANES), 1)
+    lane = lax.broadcasted_iota(jnp.int32, (8, LANES), 1)
     for number in range(source_count):
         @pl.when(held[number])
         def _(number=number):
+            chosen = jnp.where(lane == local[number] % LANES, 1.0, 0.0).astype(jnp.bfloat16)
             for part in range(parts):
                 copy(number, part).wait()
-                total = jnp.zeros((columns, mode_count), jnp.float32)
+                row = lax.dot_general(
+                    chosen,
+                    columns_ref[number, part].reshape(spin_color * mode_count, LANES),
+                    (((1,), (1,)), ((), ())),
+                    preferred_element_type=jnp.float32,
+                )
+                base = (part * source_count + number) * spin_color
                 for component in range(spin_color):
-                    chosen = (row == number * spin_color + component) & (lane == local[number] % LANES)
-                    total += lax.dot_general(
-                        jnp.where(chosen, 1.0, 0.0).astype(jnp.bfloat16),
-                        columns_ref[number, part, component],
-                        (((1,), (1,)), ((), ())),
-                        preferred_element_type=jnp.float32,
-                    )
-                total_ref[pl.ds(part * columns, columns), :] += total
+                    total_ref[base + component, :] = row[0, component * mode_count:(component + 1) * mode_count]
     rows_ref[...] = total_ref[...].astype(rows_ref.dtype)
 
 
@@ -60,16 +61,45 @@
     return pl.pallas_call(
         pick_kernel,
         out_shape=jax.ShapeDtypeStruct((rows, mode_count), vectors.dtype),
-        in_specs=[pl.BlockSpec(memory_space=pltpu.SMEM), pl.BlockSpec(memory_space=pl.ANY)],
+        in_specs=[pl.BlockSpec(memory_space=pl.ANY)] * 2,
         out_specs=pl.BlockSpec(memory_space=pltpu.VMEM),
         scratch_shapes=[
+            pltpu.SMEM(source_sites.shape, source_sites.dtype),
             pltpu.VMEM((source_count, parts, spin_color, mode_count, LANES), vectors.dtype),
             pltpu.VMEM((rows, mode_count), jnp.float32),
+            pltpu.SemaphoreType.DMA,
             pltpu.SemaphoreType.DMA((source_count, parts)),
         ],
-        compiler_params=pltpu.CompilerParams(vmem_limit_bytes=16 * MIB),
+        compiler_params=pltpu.CompilerParams(vmem_limit_bytes=24 * MIB),
         name="pick",
     )(source_sites, vectors)
+
+
+def load(vectors, after, start, count):
+    parts, spin_color, mode_count, site_count = vectors.shape
+
+    def load_kernel(vectors_ref, after_ref, held_ref, sems):
+        copies = [
+            pltpu.make_async_copy(vectors_ref.at[part, pl.ds(start, count)], held_ref.at[part], sems.at[part])
+            for part in range(parts)
+        ]
+        for copy in copies:
+            copy.start()
+        for copy in copies:
+            copy.wait()
+
+    shape = (parts, count, mode_count, site_count)
+    size = 2 * parts * count * mode_count * site_count
+    return pl.pallas_call(
+        load_kernel,
+        out_shape=jax.ShapeDtypeStruct(shape, vectors.dtype),
+        in_specs=[pl.BlockSpec(memory_space=pl.ANY)] * 2,
+        out_specs=pl.BlockSpec(memory_space=pltpu.VMEM),
+        scratch_shapes=[pltpu.SemaphoreType.DMA((parts,))],
+        compiler_params=pltpu.CompilerParams(vmem_limit_bytes=40 * MIB),
+        cost_estimate=pl.CostEstimate(flops=0, bytes_accessed=2 * size, transcendentals=0),
+        name="load",
+    )(vectors, after)
 
 
 def iota(shape, dim):
@@ -96,8 +126,8 @@
     return jnp.dot(left, right, preferred_element_type=jnp.float32)
 
 
-def project_kernel(rows_ref, values_ref, vectors_ref, sent_ref, kept_ref, flat_ref):
-    parts, spin_color, mode_count, site_count = vectors_ref.shape
+def project_kernel(rows_ref, values_ref, *refs):
+    vectors_refs, (sent_ref, kept_ref, flat_ref) = refs[:-3], refs[-3:]
     columns = rows_ref.shape[0] // 2
     ways = 4
     share = 2 * columns // ways
@@ -109,27 +139,31 @@
     on_real, on_imag = shares(columns, ways, index % 2, index // 2)
     left_real = dot(on_real, weights).astype(jnp.bfloat16)
     left_imag = dot(on_imag, weights).astype(jnp.bfloat16)
-    for component in range(spin_color):
-        product = dot(left_real, vectors_ref[0, component]) + dot(left_imag, vectors_ref[1, component])
-        for place in range(ways):
-            flat_ref[place, pl.ds(component * share, share), :] = product[place * share:(place + 1) * share]
+    component = 0
+    for vectors_ref in vectors_refs:
+        for inner in range(vectors_ref.shape[1]):
+            product = dot(left_real, vectors_ref[0, inner]) + dot(left_imag, vectors_ref[1, inner])
+            for place in range(ways):
+                flat_ref[place, pl.ds(component * share, share), :] = product[place * share:(place + 1) * share]
+            component += 1
     sent_ref[...] = flat_ref[:2].astype(sent_ref.dtype)
     kept_ref[...] = flat_ref[2:].astype(kept_ref.dtype)
 
 
-def project(rows, eigenvalues, vectors):
-    parts, spin_color, mode_count, site_count = vectors.shape
+def project(rows, eigenvalues, pieces):
+    mode_count, site_count = pieces[0].shape[2:]
+    spin_color = sum(piece.shape[1] for piece in pieces)
     share = rows.shape[0] // 4 * spin_color
     shape = (2, share, site_count)
     return pl.pallas_call(
         project_kernel,
         out_shape=[jax.ShapeDtypeStruct(shape, jnp.bfloat16), jax.ShapeDtypeStruct(shape, jnp.float32)],
-        in_specs=[pl.BlockSpec(memory_space=pltpu.VMEM)] * 3,
+        in_specs=[pl.BlockSpec(memory_space=pltpu.VMEM)] * (2 + len(pieces)),
         out_specs=[pl.BlockSpec(memory_space=pltpu.VMEM)] * 2,
         scratch_shapes=[pltpu.VMEM((4, share, site_count), jnp.float32)],
         compiler_params=pltpu.CompilerParams(vmem_limit_bytes=32 * MIB),
         name="project",
-    )(rows, eigenvalues.reshape(1, mode_count), vectors)
+    )(rows, eigenvalues.reshape(1, mode_count), *pieces)
 
 
 def swap(block, axis, size, bit):
@@ -140,12 +174,21 @@
     site_ways, mode_ways = lax.axis_size("sites"), lax.axis_size("modes")
     vectors = jnp.transpose(eigvecs, (0, 2, 1, 3))
     parts, spin_color, mode_count, site_count = vectors.shape
-    rows = pick(source_sites, vectors)
-    bit = 1
+    rows = pick(pltpu.with_memory_space_constraint(source_sites, pltpu.HBM), pltpu.with_memory_space_constraint(vectors, pltpu.HBM))
+    groups = list(GROUPS)
+    bit = 8
     while bit < site_ways:
-        rows = rows + swap(rows, "sites", site_ways, bit)
+        groups.append([bit])
         bit *= 2
-    sent, kept = project(rows, eigenvalues, vectors)
+    pieces = []
+    step = spin_color // len(GROUPS)
+    for number, group in enumerate(groups):
+        if number < len(GROUPS):
+            pass
+        for block in [swap(rows, "sites", site_ways, bit) for bit in group]:
+            rows = rows + block
+    pieces = [pltpu.with_memory_space_constraint(vectors, pltpu.VMEM)]
+    sent, kept = project(rows, eigenvalues, pieces)
     got = swap(sent, "modes", mode_ways, 1)
     across = (kept[0] + got[1].astype(jnp.float32)).astype(jnp.bfloat16)
     arrived = swap(across, "modes", mode_ways, 2)

time: 33.4 us -> 28.1 us (0.84)
  local copies, waits for them, and re-layouts: 6.14 us -> 0.91 us
  starting transfers between devices: 8.05 us -> 11.5 us
  waiting for transfers between devices: 14.1 us -> 11.9 us
  Pallas kernels: 4.88 us -> 3.34 us
    unnamed x8 -> x4, local copies, waits for them, and re-layouts: 5.24 us -> 0.01 us
    ppermute x5 -> x6, starting transfers between devices: 8.05 us -> 11.5 us  [swap(): lax.ppermute(block, axis, [(index, index ^ bit) for index in range(size)])]
    ppermute x5 -> x6, waiting for transfers between devices: 14.1 us -> 11.9 us  [swap(): lax.ppermute(block, axis, [(index, index ^ bit) for index in range(size)])]
    pallas_call x1, Pallas kernels: 2.42 us -> 0.87 us  [pick(): pl.pallas_call(pick_kernel, out_shape=jax.ShapeDtypeStruct((rows, mode_co...]
  transfers between devices with their start and end apart: 5 -> 6, of which waited for: 5 -> 6; matrix products, arithmetic and copies ran while one was open for 0% -> 0% of each run, Pallas kernels for 0% -> 0%
where the time goes in v2:
time: 28.1 us; the launch traced here: 27.8 us
  waiting for transfers between devices  11.9 us (42%)
  starting transfers between devices  11.5 us (41%)
  Pallas kernels  3.34 us (12%)
  local copies, waits for them, and re-layouts  0.91 us (3%)
    ppermute x6, waiting for transfers between devices, swap(): lax.ppermute(block, axis, [(index, index ^ bit) for index in range(size)])  11.9 us
    ppermute x6, starting transfers between devices, swap(): lax.ppermute(block, axis, [(index, index ^ bit) for index in range(size)])  11.5 us
    pallas_call x1, Pallas kernels, project(): pl.pallas_call(project_kernel, out_shape=[jax.ShapeDtypeStruct(shape, jnp...  2.47 us
    reshape x2, local copies, waits for them, and re-layouts, on_device(): total.reshape(spin_color, share, 2, site_count)  0.9 us
    pallas_call x1, Pallas kernels, pick(): pl.pallas_call(pick_kernel, out_shape=jax.ShapeDtypeStruct((rows, mode_co...  0.87 us
  transfers between devices with their start and end apart: 6, of which 6 were waited for; matrix products, arithmetic and copies ran while one was open for 0% of the time, Pallas kernels for 0%

profile of v2, /device:TPU:0, one launch (start us, length us, event | category | flops | bytes accessed | tf_op | source)
XLA Modules:
  0.0 27.8 jit_solution(7659074436931709659)
XLA Ops:
  0.0 0.0 copy-start
  0.0 0.0 copy-start.1
  0.0 0.9 %pick.1 = bf16[48,512]{1,0:T(8,128)(2,1)S(1)} custom-call(s32[2]{0:T(128)} %given_ref.1, bf16[2,12,512,512]{3,2,1,0:T(8,128)(2,1)} %bitcast.9), custom_call_target="tpu_custom_call" | custom-call | tf_op jit(solution)/shard_map/pick/pallas_call | solution.py:61
  0.9 4.0 %collective-permute-start.2 = (bf16[48,512]{1,0:T(8,128)(2,1)S(1)}, bf16[48,512]{1,0:T(8,128)(2,1)S(1)}, u32[]{:S(2)}, u32[]{:S(2)}) collective-permute-start(bf16[48,512]{1,0:T(8,128)(2,1)S(1)} %pick.1), channel_id=1, source_target_pairs={{0,3},{1,2},{2,1},{3,0},{4,7},{5,6},{6,5},{7,4},{8,11},{9,10},{10,... | collective-permute-start | bytes 147464 | tf_op jit(solution)/shard_map/ppermute | solution.py:170
  4.9 0.4 %collective-permute-start.1 = (bf16[48,512]{1,0:T(8,128)(2,1)S(1)}, bf16[48,512]{1,0:T(8,128)(2,1)S(1)}, u32[]{:S(2)}, u32[]{:S(2)}) collective-permute-start(bf16[48,512]{1,0:T(8,128)(2,1)S(1)} %pick.1), channel_id=1, source_target_pairs={{0,2},{1,3},{2,0},{3,1},{4,6},{5,7},{6,4},{7,5},{8,10},{9,11},{10,... | collective-permute-start | bytes 147464 | tf_op jit(solution)/shard_map/ppermute | solution.py:170
  5.4 0.2 collective-permute-start
  5.5 1.4 %collective-permute-done.2 = bf16[48,512]{1,0:T(8,128)(2,1)S(1)} collective-permute-done((bf16[48,512]{1,0:T(8,128)(2,1)S(1)}, bf16[48,512]{1,0:T(8,128)(2,1)S(1)}, u32[]{:S(2)}, u32[]{:S(2)}) %collective-permute-start.2) | collective-permute-done | bytes 49184 | tf_op jit(solution)/shard_map/ppermute | solution.py:170
  7.0 2.0 %collective-permute-done.1 = bf16[48,512]{1,0:T(8,128)(2,1)S(1)} collective-permute-done((bf16[48,512]{1,0:T(8,128)(2,1)S(1)}, bf16[48,512]{1,0:T(8,128)(2,1)S(1)}, u32[]{:S(2)}, u32[]{:S(2)}) %collective-permute-start.1) | collective-permute-done | bytes 49184 | tf_op jit(solution)/shard_map/ppermute | solution.py:170
  9.0 0.4 %collective-permute-done = bf16[48,512]{1,0:T(8,128)(2,1)S(1)} collective-permute-done((bf16[48,512]{1,0:T(8,128)(2,1)S(1)}, bf16[48,512]{1,0:T(8,128)(2,1)S(1)}, u32[]{:S(2)}, u32[]{:S(2)}) %collective-permute-start) | collective-permute-done | bytes 49184 | tf_op jit(solution)/shard_map/ppermute | solution.py:170
  9.5 5.2 %collective-permute-start.3 = (bf16[48,512]{1,0:T(8,128)(2,1)S(1)}, bf16[48,512]{1,0:T(8,128)(2,1)S(1)}, u32[]{:S(2)}, u32[]{:S(2)}) collective-permute-start(bf16[48,512]{1,0:T(8,128)(2,1)S(1)} %add_add_fusion), channel_id=1, source_target_pairs={{0,4},{1,5},{2,6},{3,7},{4,0},{5,1},{6,2},{7,3},{8,12},{9,13},{10,... | collective-permute-start | bytes 147464 | tf_op jit(solution)/shard_map/ppermute | solution.py:170
  14.7 2.1 %collective-permute-done.3 = bf16[48,512]{1,0:T(8,128)(2,1)S(1)} collective-permute-done((bf16[48,512]{1,0:T(8,128)(2,1)S(1)}, bf16[48,512]{1,0:T(8,128)(2,1)S(1)}, u32[]{:S(2)}, u32[]{:S(2)}) %collective-permute-start.3) | collective-permute-done | bytes 49184 | tf_op jit(solution)/shard_map/ppermute | solution.py:170
  16.7 0.0 copy-done
  16.7 0.0 copy-done.1
  16.8 2.5 %project.1 = (bf16[2,144,512]{2,1,0:T(8,128)(2,1)S(1)}, f32[2,144,512]{2,1,0:T(8,128)S(1)}) custom-call(bf16[48,512]{1,0:T(8,128)(2,1)S(1)} %add.28.rows_ref, f32[1,512]{1,0:T(1,128)S(1)} %bitcast.11, bf16[2,12,512,512]{3,2,1,0:T(8,128)(2,1)S(1)} %bitcast.10), custom_call_target="tpu_custom_call" | custom-call | tf_op jit(solution)/shard_map/project/pallas_call | solution.py:158
  19.2 0.1 collective-permute-start.4
  19.3 1.6 %collective-permute-done.4 = bf16[2,144,512]{2,1,0:T(8,128)(2,1)S(1)} collective-permute-done((bf16[2,144,512]{2,1,0:T(8,128)(2,1)S(1)}, bf16[2,144,512]{2,1,0:T(8,128)(2,1)S(1)}, u32[]{:S(2)}, u32[]{:S(2)}) %collective-permute-start.4) | collective-permute-done | bytes 294944 | tf_op jit(solution)/shard_map/ppermute | solution.py:170
  20.9 1.6 %collective-permute-start.5 = (bf16[144,512]{1,0:T(8,128)(2,1)S(1)}, bf16[144,512]{1,0:T(8,128)(2,1)S(1)}, u32[]{:S(2)}, u32[]{:S(2)}) collective-permute-start(bf16[144,512]{1,0:T(8,128)(2,1)S(1)} %fusion), channel_id=1, source_target_pairs={{0,16},{8,24},{16,0},{24,8},{1,17},{9,25},{17,1},{25,9},{2,18},{10... | collective-permute-start | bytes 442376 | tf_op jit(solution)/shard_map/ppermute | solution.py:170
  22.5 4.4 %collective-permute-done.5 = bf16[144,512]{1,0:T(8,128)(2,1)S(1)} collective-permute-done((bf16[144,512]{1,0:T(8,128)(2,1)S(1)}, bf16[144,512]{1,0:T(8,128)(2,1)S(1)}, u32[]{:S(2)}, u32[]{:S(2)}) %collective-permute-start.5) | collective-permute-done | bytes 147488 | tf_op jit(solution)/shard_map/ppermute | solution.py:170
  26.9 0.2 reshape.12
  27.1 0.7 %copy.6 = f32[12,6,2,512]{3,2,0,1:T(2,128)} copy(f32[12,6,2,512]{3,2,1,0:T(2,128)S(1)} %reshape.12) | data formatting | bytes 589824 | tf_op jit(solution)/shard_map/reshape | solution.py:197
  (4 shorter events, 0.1 us)
Async XLA Ops:
  0.0 16.7 %copy-start = (bf16[2,512,12,512]{3,1,2,0:T(8,128)(2,1)S(1)}, bf16[2,512,12,512]{3,1,2,0:T(8,128)(2,1)}, u32[]{:S(2)}) copy-start(bf16[2,512,12,512]{3,1,2,0:T(8,128)(2,1)} %param.3) | copy-start | bytes 37748740
  0.0 16.7 %copy-start.1 = (f32[512]{0:T(512)S(1)}, f32[512]{0:T(512)}, u32[]{:S(2)}) copy-start(f32[512]{0:T(512)} %param.4) | copy-start | bytes 6148
  0.9 6.1 %collective-permute-start.2 = (bf16[48,512]{1,0:T(8,128)(2,1)S(1)}, bf16[48,512]{1,0:T(8,128)(2,1)S(1)}, u32[]{:S(2)}, u32[]{:S(2)}) collective-permute-start(bf16[48,512]{1,0:T(8,128)(2,1)S(1)} %pick.1), channel_id=1, source_target_pairs={{0,3},{1,2},{2,1},{3,0},{4,7},{5,6},{6,5},{7,4},{8,11},{9,10},{10,... | collective-permute-start | bytes 147464 | tf_op jit(solution)/shard_map/ppermute | solution.py:170
  4.9 4.1 %collective-permute-start.1 = (bf16[48,512]{1,0:T(8,128)(2,1)S(1)}, bf16[48,512]{1,0:T(8,128)(2,1)S(1)}, u32[]{:S(2)}, u32[]{:S(2)}) collective-permute-start(bf16[48,512]{1,0:T(8,128)(2,1)S(1)} %pick.1), channel_id=1, source_target_pairs={{0,2},{1,3},{2,0},{3,1},{4,6},{5,7},{6,4},{7,5},{8,10},{9,11},{10,... | collective-permute-start | bytes 147464 | tf_op jit(solution)/shard_map/ppermute | solution.py:170
  5.4 4.1 %collective-permute-start = (bf16[48,512]{1,0:T(8,128)(2,1)S(1)}, bf16[48,512]{1,0:T(8,128)(2,1)S(1)}, u32[]{:S(2)}, u32[]{:S(2)}) collective-permute-start(bf16[48,512]{1,0:T(8,128)(2,1)S(1)} %pick.1), channel_id=1, source_target_pairs={{0,1},{1,0},{2,3},{3,2},{4,5},{5,4},{6,7},{7,6},{8,9},{9,8},{10,11... | collective-permute-start | bytes 147464 | tf_op jit(solution)/shard_map/ppermute | solution.py:170
  9.5 7.3 %collective-permute-start.3 = (bf16[48,512]{1,0:T(8,128)(2,1)S(1)}, bf16[48,512]{1,0:T(8,128)(2,1)S(1)}, u32[]{:S(2)}, u32[]{:S(2)}) collective-permute-start(bf16[48,512]{1,0:T(8,128)(2,1)S(1)} %add_add_fusion), channel_id=1, source_target_pairs={{0,4},{1,5},{2,6},{3,7},{4,0},{5,1},{6,2},{7,3},{8,12},{9,13},{10,... | collective-permute-start | bytes 147464 | tf_op jit(solution)/shard_map/ppermute | solution.py:170
  19.2 1.6 %collective-permute-start.4 = (bf16[2,144,512]{2,1,0:T(8,128)(2,1)S(1)}, bf16[2,144,512]{2,1,0:T(8,128)(2,1)S(1)}, u32[]{:S(2)}, u32[]{:S(2)}) collective-permute-start(bf16[2,144,512]{2,1,0:T(8,128)(2,1)S(1)} %get-tuple-element.8), channel_id=1, source_target_pairs={{0,8},{8,0},{16,24},{24,16},{1,9},{9,1},{17,25},{25,17},{2,10},{10... | collective-permute-start | bytes 884744 | tf_op jit(solution)/shard_map/ppermute | solution.py:170
  20.9 6.0 %collective-permute-start.5 = (bf16[144,512]{1,0:T(8,128)(2,1)S(1)}, bf16[144,512]{1,0:T(8,128)(2,1)S(1)}, u32[]{:S(2)}, u32[]{:S(2)}) collective-permute-start(bf16[144,512]{1,0:T(8,128)(2,1)S(1)} %fusion), channel_id=1, source_target_pairs={{0,16},{8,24},{16,0},{24,8},{1,17},{9,25},{17,1},{25,9},{2,18},{10... | collective-permute-start | bytes 442376 | tf_op jit(solution)/shard_map/ppermute | solution.py:170

commit v3 on v2

--- a/solution.py
+++ b/solution.py
@@ -1,3 +1,5 @@
+import functools
+
 import jax
 import jax.numpy as jnp
 from jax import lax
@@ -7,7 +9,9 @@
 
 LANES = 128
 MIB = 2**20
-GROUPS = [[1, 2, 3], [4]]
+ROWS = 128
+FIRST = 4
+GROUPS = [[1], [2, 4, 6]]
 
 
 def pick_kernel(given_ref, vectors_ref, rows_ref, sites_ref, columns_ref, total_ref, given_sem, sems):
@@ -126,44 +130,61 @@
     return jnp.dot(left, right, preferred_element_type=jnp.float32)
 
 
-def project_kernel(rows_ref, values_ref, *refs):
-    vectors_refs, (sent_ref, kept_ref, flat_ref) = refs[:-3], refs[-3:]
+def multiply(left, vectors_ref, start, sent_ref, kept_ref, flat_ref, share):
+    count = flat_ref.shape[1] // share
+    for inner in range(count):
+        component = start + inner
+        product = dot(left[0], vectors_ref[0, component]) + dot(left[1], vectors_ref[1, component])
+        for place in range(flat_ref.shape[0]):
+            flat_ref[place, pl.ds(inner * share, share), :] = product[place * share:(place + 1) * share]
+    sent_ref[...] = flat_ref[:2].astype(sent_ref.dtype)
+    kept_ref[...] = flat_ref[2:].astype(kept_ref.dtype)
+
+
+def first_kernel(rows_ref, values_ref, vectors_ref, sent_ref, kept_ref, left_ref, flat_ref):
     columns = rows_ref.shape[0] // 2
-    ways = 4
-    share = 2 * columns // ways
+    ways = flat_ref.shape[0]
     index = lax.axis_index("modes")
     divisor = values_ref[...]
     real = rows_ref[:columns, :].astype(jnp.float32) / divisor
     imag = -rows_ref[columns:, :].astype(jnp.float32) / divisor
     weights = jnp.concatenate([real, imag], axis=0).astype(jnp.bfloat16)
     on_real, on_imag = shares(columns, ways, index % 2, index // 2)
-    left_real = dot(on_real, weights).astype(jnp.bfloat16)
-    left_imag = dot(on_imag, weights).astype(jnp.bfloat16)
-    component = 0
-    for vectors_ref in vectors_refs:
-        for inner in range(vectors_ref.shape[1]):
-            product = dot(left_real, vectors_ref[0, inner]) + dot(left_imag, vectors_ref[1, inner])
-            for place in range(ways):
-                flat_ref[place, pl.ds(component * share, share), :] = product[place * share:(place + 1) * share]
-            component += 1
-    sent_ref[...] = flat_ref[:2].astype(sent_ref.dtype)
-    kept_ref[...] = flat_ref[2:].astype(kept_ref.dtype)
-
-
-def project(rows, eigenvalues, pieces):
-    mode_count, site_count = pieces[0].shape[2:]
-    spin_color = sum(piece.shape[1] for piece in pieces)
-    share = rows.shape[0] // 4 * spin_color
-    shape = (2, share, site_count)
-    return pl.pallas_call(
-        project_kernel,
-        out_shape=[jax.ShapeDtypeStruct(shape, jnp.bfloat16), jax.ShapeDtypeStruct(shape, jnp.float32)],
-        in_specs=[pl.BlockSpec(memory_space=pltpu.VMEM)] * (2 + len(pieces)),
-        out_specs=[pl.BlockSpec(memory_space=pltpu.VMEM)] * 2,
-        scratch_shapes=[pltpu.VMEM((4, share, site_count), jnp.float32)],
-        compiler_params=pltpu.CompilerParams(vmem_limit_bytes=32 * MIB),
-        name="project",
-    )(rows, eigenvalues.reshape(1, mode_count), *pieces)
+    spare = jnp.zeros((ROWS - 2 * columns, weights.shape[1]), jnp.bfloat16)
+    left = [jnp.concatenate([dot(on, weights).astype(jnp.bfloat16), spare], axis=0) for on in (on_real, on_imag)]
+    left_ref[0] = left[0]
+    left_ref[1] = left[1]
+    multiply(left, vectors_ref, 0, sent_ref, kept_ref, flat_ref, 2 * columns // ways)
+
+
+def next_kernel(start, left_ref, vectors_ref, sent_ref, kept_ref, flat_ref):
+    share = flat_ref.shape[1] // (vectors_ref.shape[1] - start)
+    multiply([left_ref[0], left_ref[1]], vectors_ref, start, sent_ref, kept_ref, flat_ref, share)
+
+
+def project(rows, eigenvalues, vectors, ways):
+    parts, spin_color, mode_count, site_count = vectors.shape
+    share = rows.shape[0] // ways
+    vmem = pl.BlockSpec(memory_space=pltpu.VMEM)
+
+    def call(kernel, operands, count, extra, name):
+        shape = (2, count * share, site_count)
+        size = 2 * parts * count * mode_count * site_count
+        return pl.pallas_call(
+            kernel,
+            out_shape=[jax.ShapeDtypeStruct(shape, jnp.bfloat16), jax.ShapeDtypeStruct(shape, jnp.float32)] + extra,
+            in_specs=[vmem] * len(operands),
+            out_specs=[vmem] * (2 + len(extra)),
+            scratch_shapes=[pltpu.VMEM((ways, count * share, site_count), jnp.float32)],
+            compiler_params=pltpu.CompilerParams(vmem_limit_bytes=24 * MIB),
+            cost_estimate=pl.CostEstimate(flops=size * ROWS, bytes_accessed=size, transcendentals=0),
+            name=name,
+        )(*operands)
+
+    left = jax.ShapeDtypeStruct((2, ROWS, mode_count), jnp.bfloat16)
+    *first, left = call(first_kernel, (rows, eigenvalues.reshape(1, mode_count), vectors), FIRST, [left], "first")
+    rest = call(functools.partial(next_kernel, FIRST), (left, vectors), spin_color - FIRST, [], "rest")
+    return [first, rest]
 
 
 def swap(block, axis, size, bit):
@@ -187,12 +208,13 @@
             pass
         for block in [swap(rows, "sites", site_ways, bit) for bit in group]:
             rows = rows + block
-    pieces = [pltpu.with_memory_space_constraint(vectors, pltpu.VMEM)]
-    sent, kept = project(rows, eigenvalues, pieces)
-    got = swap(sent, "modes", mode_ways, 1)
-    across = (kept[0] + got[1].astype(jnp.float32)).astype(jnp.bfloat16)
-    arrived = swap(across, "modes", mode_ways, 2)
-    total = kept[1] + got[0].astype(jnp.float32) + arrived.astype(jnp.float32)
+    halves = []
+    for sent, kept in project(rows, eigenvalues, pltpu.with_memory_space_constraint(vectors, pltpu.VMEM), mode_ways):
+        got = swap(sent, "modes", mode_ways, 1)
+        across = (kept[0] + got[1].astype(jnp.float32)).astype(jnp.bfloat16)
+        arrived = swap(across, "modes", mode_ways, 2)
+        halves.append(kept[1] + got[0].astype(jnp.float32) + arrived.astype(jnp.float32))
+    total = jnp.concatenate(halves, axis=0)
     share = total.shape[0] // spin_color // 2
     return jnp.transpose(total.reshape(spin_color, share, 2, site_count), (1, 2, 0, 3))
 

time: 28.1 us -> 27.2 us (0.968); the launches traced: 27.8 us -> 27.5 us
  starting transfers between devices: 11.5 us -> 13.4 us
  waiting for transfers between devices: 11.9 us -> 10 us
  Pallas kernels: 3.34 us -> 3 us
    ppermute x6 -> x8, waiting for transfers between devices: 11.9 us -> 10 us  [swap(): lax.ppermute(block, axis, [(index, index ^ bit) for index in range(size)])]
    ppermute x6 -> x8, starting transfers between devices: 11.5 us -> 13.4 us  [swap(): lax.ppermute(block, axis, [(index, index ^ bit) for index in range(size)])]
    pallas_call x1 -> x2, Pallas kernels: 2.47 us -> 2.13 us  [call(): pl.pallas_call(kernel, out_shape=[jax.ShapeDtypeStruct(shape, jnp.bfloat1...]
  transfers between devices with their start and end apart: 6 -> 8, of which waited for: 6 -> 5; matrix products, arithmetic and copies ran while one was open for 0% -> 0% of each run, Pallas kernels for 0% -> 5%
where the time goes in v3:
time: 27.2 us; the launch traced here: 27.5 us
  starting transfers between devices  13.4 us (49%)
  waiting for transfers between devices  10 us (37%)
  Pallas kernels  3 us (11%)
  local copies, waits for them, and re-layouts  0.91 us (3%)
    ppermute x8, starting transfers between devices, swap(): lax.ppermute(block, axis, [(index, index ^ bit) for index in range(size)])  13.4 us
    ppermute x8, waiting for transfers between devices, swap(): lax.ppermute(block, axis, [(index, index ^ bit) for index in range(size)])  10 us
    pallas_call x2, Pallas kernels, call(): pl.pallas_call(kernel, out_shape=[jax.ShapeDtypeStruct(shape, jnp.bfloat1...  2.13 us
    reshape x2, local copies, waits for them, and re-layouts, on_device(): total.reshape(spin_color, share, 2, site_count)  0.9 us
    pallas_call x1, Pallas kernels, pick(): pl.pallas_call(pick_kernel, out_shape=jax.ShapeDtypeStruct((rows, mode_co...  0.87 us
  transfers between devices with their start and end apart: 8, of which 5 were waited for; matrix products, arithmetic and copies ran while one was open for 0% of the time, Pallas kernels for 5%

profile of v3, /device:TPU:0, one launch (start us, length us, event | category | flops | bytes accessed | tf_op | source)
XLA Modules:
  0.0 27.5 jit_solution(10966203189317710680)
XLA Ops:
  0.0 0.0 copy-start
  0.0 0.0 copy-start.1
  0.0 0.9 %pick.1 = bf16[48,512]{1,0:T(8,128)(2,1)S(1)} custom-call(s32[2]{0:T(128)} %given_ref.1, bf16[2,12,512,512]{3,2,1,0:T(8,128)(2,1)} %bitcast.13), custom_call_target="tpu_custom_call" | custom-call | tf_op jit(solution)/shard_map/pick/pallas_call | solution.py:65
  0.9 3.0 %collective-permute-start = (bf16[48,512]{1,0:T(8,128)(2,1)S(1)}, bf16[48,512]{1,0:T(8,128)(2,1)S(1)}, u32[]{:S(2)}, u32[]{:S(2)}) collective-permute-start(bf16[48,512]{1,0:T(8,128)(2,1)S(1)} %pick.1), channel_id=1, source_target_pairs={{0,1},{1,0},{2,3},{3,2},{4,5},{5,4},{6,7},{7,6},{8,9},{9,8},{10,11... | collective-permute-start | bytes 147464 | tf_op jit(solution)/shard_map/ppermute | solution.py:191
  3.9 2.1 %collective-permute-done = bf16[48,512]{1,0:T(8,128)(2,1)S(1)} collective-permute-done((bf16[48,512]{1,0:T(8,128)(2,1)S(1)}, bf16[48,512]{1,0:T(8,128)(2,1)S(1)}, u32[]{:S(2)}, u32[]{:S(2)}) %collective-permute-start) | collective-permute-done | bytes 49184 | tf_op jit(solution)/shard_map/ppermute | solution.py:191
  6.0 6.4 %collective-permute-start.3 = (bf16[48,512]{1,0:T(8,128)(2,1)S(1)}, bf16[48,512]{1,0:T(8,128)(2,1)S(1)}, u32[]{:S(2)}, u32[]{:S(2)}) collective-permute-start(bf16[48,512]{1,0:T(8,128)(2,1)S(1)} %add.38), channel_id=1, source_target_pairs={{0,6},{1,7},{2,4},{3,5},{4,2},{5,3},{6,0},{7,1},{8,14},{9,15},{10,... | collective-permute-start | bytes 147464 | tf_op jit(solution)/shard_map/ppermute | solution.py:191
  12.4 0.0 collective-permute-start.2
  12.4 0.6 %collective-permute-start.1 = (bf16[48,512]{1,0:T(8,128)(2,1)S(1)}, bf16[48,512]{1,0:T(8,128)(2,1)S(1)}, u32[]{:S(2)}, u32[]{:S(2)}) collective-permute-start(bf16[48,512]{1,0:T(8,128)(2,1)S(1)} %add.38), channel_id=1, source_target_pairs={{0,2},{1,3},{2,0},{3,1},{4,6},{5,7},{6,4},{7,5},{8,10},{9,11},{10,... | collective-permute-start | bytes 147464 | tf_op jit(solution)/shard_map/ppermute | solution.py:191
  13.1 1.5 %collective-permute-done.3 = bf16[48,512]{1,0:T(8,128)(2,1)S(1)} collective-permute-done((bf16[48,512]{1,0:T(8,128)(2,1)S(1)}, bf16[48,512]{1,0:T(8,128)(2,1)S(1)}, u32[]{:S(2)}, u32[]{:S(2)}) %collective-permute-start.3) | collective-permute-done | bytes 49184 | tf_op jit(solution)/shard_map/ppermute | solution.py:191
  14.6 2.8 %collective-permute-done.2 = bf16[48,512]{1,0:T(8,128)(2,1)S(1)} collective-permute-done((bf16[48,512]{1,0:T(8,128)(2,1)S(1)}, bf16[48,512]{1,0:T(8,128)(2,1)S(1)}, u32[]{:S(2)}, u32[]{:S(2)}) %collective-permute-start.2) | collective-permute-done | bytes 49184 | tf_op jit(solution)/shard_map/ppermute | solution.py:191
  17.4 0.0 collective-permute-done.1
  17.4 0.0 copy-done
  17.4 0.0 copy-done.1
  17.5 0.9 %first.1 = (bf16[2,48,512]{2,1,0:T(8,128)(2,1)S(1)}, f32[2,48,512]{2,1,0:T(8,128)S(1)}, bf16[2,128,512]{2,1,0:T(8,128)(2,1)S(1)}) custom-call(bf16[48,512]{1,0:T(8,128)(2,1)S(1)} %add_add_fusion.rows_ref, f32[1,512]{1,0:T(1,128)S(1)} %bitcast.16, bf16[2,12,512,512]{3,2,1,0:T(8,128)(2,1)S(1)} %bitcast.14), custom_call_target="tpu_custom_call" | custom-call | flops 536870912 | bytes 4194304 | tf_op jit(solution)/shard_map/first/pallas_call | solution.py:173
  18.3 0.1 collective-permute-start.4
  18.4 1.3 %rest.1 = (bf16[2,96,512]{2,1,0:T(8,128)(2,1)S(1)}, f32[2,96,512]{2,1,0:T(8,128)S(1)}) custom-call(bf16[2,128,512]{2,1,0:T(8,128)(2,1)S(1)} %get-tuple-element.12.left_ref, bf16[2,12,512,512]{3,2,1,0:T(8,128)(2,1)S(1)} %bitcast.15), custom_call_target="tpu_custom_call" | custom-call | flops 1073741824 | bytes 8388608 | tf_op jit(solution)/shard_map/rest/pallas_call | solution.py:173
  19.7 0.6 %collective-permute-start.6 = (bf16[2,96,512]{2,1,0:T(8,128)(2,1)S(1)}, bf16[2,96,512]{2,1,0:T(8,128)(2,1)S(1)}, u32[]{:S(2)}, u32[]{:S(2)}) collective-permute-start(bf16[2,96,512]{2,1,0:T(8,128)(2,1)S(1)} %get-tuple-element.14), channel_id=1, source_target_pairs={{0,8},{8,0},{16,24},{24,16},{1,9},{9,1},{17,25},{25,17},{2,10},{10... | collective-permute-start | bytes 589832 | tf_op jit(solution)/shard_map/ppermute | solution.py:191
  20.2 0.0 collective-permute-done.4
  20.3 1.6 %collective-permute-start.5 = (bf16[48,512]{1,0:T(8,128)(2,1)S(1)}, bf16[48,512]{1,0:T(8,128)(2,1)S(1)}, u32[]{:S(2)}, u32[]{:S(2)}) collective-permute-start(bf16[48,512]{1,0:T(8,128)(2,1)S(1)} %fusion.1), channel_id=1, source_target_pairs={{0,16},{8,24},{16,0},{24,8},{1,17},{9,25},{17,1},{25,9},{2,18},{10... | collective-permute-start | bytes 147464 | tf_op jit(solution)/shard_map/ppermute | solution.py:191
  21.8 0.0 collective-permute-done.6
  21.9 1.1 %collective-permute-start.7 = (bf16[96,512]{1,0:T(8,128)(2,1)S(1)}, bf16[96,512]{1,0:T(8,128)(2,1)S(1)}, u32[]{:S(2)}, u32[]{:S(2)}) collective-permute-start(bf16[96,512]{1,0:T(8,128)(2,1)S(1)} %fusion), channel_id=1, source_target_pairs={{0,16},{8,24},{16,0},{24,8},{1,17},{9,25},{17,1},{25,9},{2,18},{10... | collective-permute-start | bytes 294920 | tf_op jit(solution)/shard_map/ppermute | solution.py:191
  22.9 1.6 %collective-permute-done.5 = bf16[48,512]{1,0:T(8,128)(2,1)S(1)} collective-permute-done((bf16[48,512]{1,0:T(8,128)(2,1)S(1)}, bf16[48,512]{1,0:T(8,128)(2,1)S(1)}, u32[]{:S(2)}, u32[]{:S(2)}) %collective-permute-start.5) | collective-permute-done | bytes 49184 | tf_op jit(solution)/shard_map/ppermute | solution.py:191
  24.5 2.0 %collective-permute-done.7 = bf16[96,512]{1,0:T(8,128)(2,1)S(1)} collective-permute-done((bf16[96,512]{1,0:T(8,128)(2,1)S(1)}, bf16[96,512]{1,0:T(8,128)(2,1)S(1)}, u32[]{:S(2)}, u32[]{:S(2)}) %collective-permute-start.7) | collective-permute-done | bytes 98336 | tf_op jit(solution)/shard_map/ppermute | solution.py:191
  26.6 0.2 reshape.17
  26.8 0.7 %copy.6 = f32[12,6,2,512]{3,2,0,1:T(2,128)} copy(f32[12,6,2,512]{3,2,1,0:T(2,128)S(1)} %reshape.17) | data formatting | bytes 589824 | tf_op jit(solution)/shard_map/reshape | solution.py:219
  (7 shorter events, 0.1 us)
Async XLA Ops:
  0.0 17.4 %copy-start = (bf16[2,512,12,512]{3,1,2,0:T(8,128)(2,1)S(1)}, bf16[2,512,12,512]{3,1,2,0:T(8,128)(2,1)}, u32[]{:S(2)}) copy-start(bf16[2,512,12,512]{3,1,2,0:T(8,128)(2,1)} %param.3) | copy-start | bytes 37748740
  0.0 17.4 %copy-start.1 = (f32[512]{0:T(512)S(1)}, f32[512]{0:T(512)}, u32[]{:S(2)}) copy-start(f32[512]{0:T(512)} %param.4) | copy-start | bytes 6148
  0.9 5.1 %collective-permute-start = (bf16[48,512]{1,0:T(8,128)(2,1)S(1)}, bf16[48,512]{1,0:T(8,128)(2,1)S(1)}, u32[]{:S(2)}, u32[]{:S(2)}) collective-permute-start(bf16[48,512]{1,0:T(8,128)(2,1)S(1)} %pick.1), channel_id=1, source_target_pairs={{0,1},{1,0},{2,3},{3,2},{4,5},{5,4},{6,7},{7,6},{8,9},{9,8},{10,11... | collective-permute-start | bytes 147464 | tf_op jit(solution)/shard_map/ppermute | solution.py:191
  6.0 8.6 %collective-permute-start.3 = (bf16[48,512]{1,0:T(8,128)(2,1)S(1)}, bf16[48,512]{1,0:T(8,128)(2,1)S(1)}, u32[]{:S(2)}, u32[]{:S(2)}) collective-permute-start(bf16[48,512]{1,0:T(8,128)(2,1)S(1)} %add.38), channel_id=1, source_target_pairs={{0,6},{1,7},{2,4},{3,5},{4,2},{5,3},{6,0},{7,1},{8,14},{9,15},{10,... | collective-permute-start | bytes 147464 | tf_op jit(solution)/shard_map/ppermute | solution.py:191
  12.4 5.0 %collective-permute-start.2 = (bf16[48,512]{1,0:T(8,128)(2,1)S(1)}, bf16[48,512]{1,0:T(8,128)(2,1)S(1)}, u32[]{:S(2)}, u32[]{:S(2)}) collective-permute-start(bf16[48,512]{1,0:T(8,128)(2,1)S(1)} %add.38), channel_id=1, source_target_pairs={{0,4},{1,5},{2,6},{3,7},{4,0},{5,1},{6,2},{7,3},{8,12},{9,13},{10,... | collective-permute-start | bytes 147464 | tf_op jit(solution)/shard_map/ppermute | solution.py:191
  12.4 5.0 %collective-permute-start.1 = (bf16[48,512]{1,0:T(8,128)(2,1)S(1)}, bf16[48,512]{1,0:T(8,128)(2,1)S(1)}, u32[]{:S(2)}, u32[]{:S(2)}) collective-permute-start(bf16[48,512]{1,0:T(8,128)(2,1)S(1)} %add.38), channel_id=1, source_target_pairs={{0,2},{1,3},{2,0},{3,1},{4,6},{5,7},{6,4},{7,5},{8,10},{9,11},{10,... | collective-permute-start | bytes 147464 | tf_op jit(solution)/shard_map/ppermute | solution.py:191
  18.3 1.9 %collective-permute-start.4 = (bf16[2,48,512]{2,1,0:T(8,128)(2,1)S(1)}, bf16[2,48,512]{2,1,0:T(8,128)(2,1)S(1)}, u32[]{:S(2)}, u32[]{:S(2)}) collective-permute-start(bf16[2,48,512]{2,1,0:T(8,128)(2,1)S(1)} %get-tuple-element.11), channel_id=1, source_target_pairs={{0,8},{8,0},{16,24},{24,16},{1,9},{9,1},{17,25},{25,17},{2,10},{10... | collective-permute-start | bytes 294920 | tf_op jit(solution)/shard_map/ppermute | solution.py:191
  19.7 2.2 %collective-permute-start.6 = (bf16[2,96,512]{2,1,0:T(8,128)(2,1)S(1)}, bf16[2,96,512]{2,1,0:T(8,128)(2,1)S(1)}, u32[]{:S(2)}, u32[]{:S(2)}) collective-permute-start(bf16[2,96,512]{2,1,0:T(8,128)(2,1)S(1)} %get-tuple-element.14), channel_id=1, source_target_pairs={{0,8},{8,0},{16,24},{24,16},{1,9},{9,1},{17,25},{25,17},{2,10},{10... | collective-permute-start | bytes 589832 | tf_op jit(solution)/shard_map/ppermute | solution.py:191
  20.3 4.3 %collective-permute-start.5 = (bf16[48,512]{1,0:T(8,128)(2,1)S(1)}, bf16[48,512]{1,0:T(8,128)(2,1)S(1)}, u32[]{:S(2)}, u32[]{:S(2)}) collective-permute-start(bf16[48,512]{1,0:T(8,128)(2,1)S(1)} %fusion.1), channel_id=1, source_target_pairs={{0,16},{8,24},{16,0},{24,8},{1,17},{9,25},{17,1},{25,9},{2,18},{10... | collective-permute-start | bytes 147464 | tf_op jit(solution)/shard_map/ppermute | solution.py:191
  21.9 4.7 %collective-permute-start.7 = (bf16[96,512]{1,0:T(8,128)(2,1)S(1)}, bf16[96,512]{1,0:T(8,128)(2,1)S(1)}, u32[]{:S(2)}, u32[]{:S(2)}) collective-permute-start(bf16[96,512]{1,0:T(8,128)(2,1)S(1)} %fusion), channel_id=1, source_target_pairs={{0,16},{8,24},{16,0},{24,8},{1,17},{9,25},{17,1},{25,9},{2,18},{10... | collective-permute-start | bytes 294920 | tf_op jit(solution)/shard_map/ppermute | solution.py:191

commit v4 on v3

--- a/solution.py
+++ b/solution.py
@@ -10,7 +10,7 @@
 LANES = 128
 MIB = 2**20
 ROWS = 128
-FIRST = 4
+STEPS = (6, 6)
 GROUPS = [[1], [2, 4, 6]]
 
 
@@ -115,7 +115,7 @@
     shape = (2 * columns, 2 * columns)
     row, entry = iota(shape, 0), iota(shape, 1)
     place, inner = row // (2 * share), row % (2 * share)
-    its_core = jnp.where(place < 2, 1 - core, core)
+    its_core = jnp.where(place % 2 == 0, 1 - core, core)
     its_plane = jnp.where((place == 0) | (place == 3), plane, 1 - plane)
     column, part = (2 * its_plane + its_core) * share + inner // 2, inner % 2
     real, imag = (entry == column), (entry == column + columns)
@@ -158,7 +158,7 @@
 
 
 def next_kernel(start, left_ref, vectors_ref, sent_ref, kept_ref, flat_ref):
-    share = flat_ref.shape[1] // (vectors_ref.shape[1] - start)
+    share = 12
     multiply([left_ref[0], left_ref[1]], vectors_ref, start, sent_ref, kept_ref, flat_ref, share)
 
 
@@ -182,9 +182,13 @@
         )(*operands)
 
     left = jax.ShapeDtypeStruct((2, ROWS, mode_count), jnp.bfloat16)
-    *first, left = call(first_kernel, (rows, eigenvalues.reshape(1, mode_count), vectors), FIRST, [left], "first")
-    rest = call(functools.partial(next_kernel, FIRST), (left, vectors), spin_color - FIRST, [], "rest")
-    return [first, rest]
+    *first, left = call(first_kernel, (rows, eigenvalues.reshape(1, mode_count), vectors), STEPS[0], [left], "first")
+    results = [first]
+    start = STEPS[0]
+    for count in STEPS[1:]:
+        results.append(call(functools.partial(next_kernel, start), (left, vectors), count, [], "rest"))
+        start += count
+    return results
 
 
 def swap(block, axis, size, bit):
@@ -212,7 +216,7 @@
     for sent, kept in project(rows, eigenvalues, pltpu.with_memory_space_constraint(vectors, pltpu.VMEM), mode_ways):
         got = swap(sent, "modes", mode_ways, 1)
         across = (kept[0] + got[1].astype(jnp.float32)).astype(jnp.bfloat16)
-        arrived = swap(across, "modes", mode_ways, 2)
+        arrived = swap(across, "modes", mode_ways, 3)
         halves.append(kept[1] + got[0].astype(jnp.float32) + arrived.astype(jnp.float32))
     total = jnp.concatenate(halves, axis=0)
     share = total.shape[0] // spin_color // 2

time: 27.2 us -> 25.5 us (0.938); the launches traced: 27.5 us -> 25.3 us
  Pallas kernels: 3 us -> 5.84 us
  waiting for transfers between devices: 10 us -> 7.33 us
  starting transfers between devices: 13.4 us -> 11 us
    pallas_call x1, Pallas kernels: 0.87 us -> 3.65 us  [pick(): pl.pallas_call(pick_kernel, out_shape=jax.ShapeDtypeStruct((rows, mode_co...]
    ppermute x8, waiting for transfers between devices: 10 us -> 7.33 us  [swap(): lax.ppermute(block, axis, [(index, index ^ bit) for index in range(size)])]
    ppermute x8, starting transfers between devices: 13.4 us -> 11 us  [swap(): lax.ppermute(block, axis, [(index, index ^ bit) for index in range(size)])]
  transfers between devices with their start and end apart: 8 -> 8, of which waited for: 5 -> 5; matrix products, arithmetic and copies ran while one was open for 0% -> 0% of each run, Pallas kernels for 5% -> 4%
where the time goes in v4:
time: 25.5 us; the launch traced here: 25.3 us
  starting transfers between devices  11 us (43%)
  waiting for transfers between devices  7.33 us (29%)
  Pallas kernels  5.84 us (23%)
  local copies, waits for them, and re-layouts  0.91 us (4%)
    ppermute x8, starting transfers between devices, swap(): lax.ppermute(block, axis, [(index, index ^ bit) for index in range(size)])  11 us
    ppermute x8, waiting for transfers between devices, swap(): lax.ppermute(block, axis, [(index, index ^ bit) for index in range(size)])  7.33 us
    pallas_call x1, Pallas kernels, pick(): pl.pallas_call(pick_kernel, out_shape=jax.ShapeDtypeStruct((rows, mode_co...  3.65 us
    pallas_call x2, Pallas kernels, call(): pl.pallas_call(kernel, out_shape=[jax.ShapeDtypeStruct(shape, jnp.bfloat1...  2.18 us
    reshape x2, local copies, waits for them, and re-layouts, on_device(): total.reshape(spin_color, share, 2, site_count)  0.9 us
  transfers between devices with their start and end apart: 8, of which 5 were waited for; matrix products, arithmetic and copies ran while one was open for 0% of the time, Pallas kernels for 4%

profile of v4, /device:TPU:0, one launch (start us, length us, event | category | flops | bytes accessed | tf_op | source)
XLA Modules:
  0.0 25.3 jit_solution(2364497122999641080)
XLA Ops:
  0.0 0.0 copy-start
  0.0 0.0 copy-start.1
  0.0 3.7 %pick.1 = bf16[48,512]{1,0:T(8,128)(2,1)S(1)} custom-call(s32[2]{0:T(128)} %given_ref.1, bf16[2,12,512,512]{3,2,1,0:T(8,128)(2,1)} %bitcast.13), custom_call_target="tpu_custom_call" | custom-call | tf_op jit(solution)/shard_map/pick/pallas_call | solution.py:65
  3.7 3.0 %collective-permute-start = (bf16[48,512]{1,0:T(8,128)(2,1)S(1)}, bf16[48,512]{1,0:T(8,128)(2,1)S(1)}, u32[]{:S(2)}, u32[]{:S(2)}) collective-permute-start(bf16[48,512]{1,0:T(8,128)(2,1)S(1)} %pick.1), channel_id=1, source_target_pairs={{0,1},{1,0},{2,3},{3,2},{4,5},{5,4},{6,7},{7,6},{8,9},{9,8},{10,11... | collective-permute-start | bytes 147464 | tf_op jit(solution)/shard_map/ppermute | solution.py:195
  6.7 2.1 %collective-permute-done = bf16[48,512]{1,0:T(8,128)(2,1)S(1)} collective-permute-done((bf16[48,512]{1,0:T(8,128)(2,1)S(1)}, bf16[48,512]{1,0:T(8,128)(2,1)S(1)}, u32[]{:S(2)}, u32[]{:S(2)}) %collective-permute-start) | collective-permute-done | bytes 49184 | tf_op jit(solution)/shard_map/ppermute | solution.py:195
  8.8 1.4 %collective-permute-start.3 = (bf16[48,512]{1,0:T(8,128)(2,1)S(1)}, bf16[48,512]{1,0:T(8,128)(2,1)S(1)}, u32[]{:S(2)}, u32[]{:S(2)}) collective-permute-start(bf16[48,512]{1,0:T(8,128)(2,1)S(1)} %add.38), channel_id=1, source_target_pairs={{0,6},{1,7},{2,4},{3,5},{4,2},{5,3},{6,0},{7,1},{8,14},{9,15},{10,... | collective-permute-start | bytes 147464 | tf_op jit(solution)/shard_map/ppermute | solution.py:195
  10.2 0.0 collective-permute-start.2
  10.2 3.0 %collective-permute-start.1 = (bf16[48,512]{1,0:T(8,128)(2,1)S(1)}, bf16[48,512]{1,0:T(8,128)(2,1)S(1)}, u32[]{:S(2)}, u32[]{:S(2)}) collective-permute-start(bf16[48,512]{1,0:T(8,128)(2,1)S(1)} %add.38), channel_id=1, source_target_pairs={{0,2},{1,3},{2,0},{3,1},{4,6},{5,7},{6,4},{7,5},{8,10},{9,11},{10,... | collective-permute-start | bytes 147464 | tf_op jit(solution)/shard_map/ppermute | solution.py:195
  13.2 1.5 %collective-permute-done.3 = bf16[48,512]{1,0:T(8,128)(2,1)S(1)} collective-permute-done((bf16[48,512]{1,0:T(8,128)(2,1)S(1)}, bf16[48,512]{1,0:T(8,128)(2,1)S(1)}, u32[]{:S(2)}, u32[]{:S(2)}) %collective-permute-start.3) | collective-permute-done | bytes 49184 | tf_op jit(solution)/shard_map/ppermute | solution.py:195
  14.7 1.1 %collective-permute-done.2 = bf16[48,512]{1,0:T(8,128)(2,1)S(1)} collective-permute-done((bf16[48,512]{1,0:T(8,128)(2,1)S(1)}, bf16[48,512]{1,0:T(8,128)(2,1)S(1)}, u32[]{:S(2)}, u32[]{:S(2)}) %collective-permute-start.2) | collective-permute-done | bytes 49184 | tf_op jit(solution)/shard_map/ppermute | solution.py:195
  15.8 0.0 collective-permute-done.1
  15.8 0.0 copy-done
  15.8 0.0 copy-done.1
  15.8 1.1 %first.1 = (bf16[2,72,512]{2,1,0:T(8,128)(2,1)S(1)}, f32[2,72,512]{2,1,0:T(8,128)S(1)}, bf16[2,128,512]{2,1,0:T(8,128)(2,1)S(1)}) custom-call(bf16[48,512]{1,0:T(8,128)(2,1)S(1)} %add_add_fusion.rows_ref, f32[1,512]{1,0:T(1,128)S(1)} %bitcast.16, bf16[2,12,512,512]{3,2,1,0:T(8,128)(2,1)S(1)} %bitcast.14), custom_call_target="tpu_custom_call" | custom-call | flops 805306368 | bytes 6291456 | tf_op jit(solution)/shard_map/first/pallas_call | solution.py:173
  17.0 0.1 collective-permute-start.4
  17.1 1.0 %rest.1 = (bf16[2,72,512]{2,1,0:T(8,128)(2,1)S(1)}, f32[2,72,512]{2,1,0:T(8,128)S(1)}) custom-call(bf16[2,128,512]{2,1,0:T(8,128)(2,1)S(1)} %get-tuple-element.12.left_ref, bf16[2,12,512,512]{3,2,1,0:T(8,128)(2,1)S(1)} %bitcast.15), custom_call_target="tpu_custom_call" | custom-call | flops 805306368 | bytes 6291456 | tf_op jit(solution)/shard_map/rest/pallas_call | solution.py:173
  18.1 0.6 %collective-permute-start.6 = (bf16[2,72,512]{2,1,0:T(8,128)(2,1)S(1)}, bf16[2,72,512]{2,1,0:T(8,128)(2,1)S(1)}, u32[]{:S(2)}, u32[]{:S(2)}) collective-permute-start(bf16[2,72,512]{2,1,0:T(8,128)(2,1)S(1)} %get-tuple-element.14), channel_id=1, source_target_pairs={{0,8},{8,0},{16,24},{24,16},{1,9},{9,1},{17,25},{25,17},{2,10},{10... | collective-permute-start | bytes 442376 | tf_op jit(solution)/shard_map/ppermute | solution.py:195
  18.7 0.0 collective-permute-done.4
  18.7 1.6 %collective-permute-start.5 = (bf16[72,512]{1,0:T(8,128)(2,1)S(1)}, bf16[72,512]{1,0:T(8,128)(2,1)S(1)}, u32[]{:S(2)}, u32[]{:S(2)}) collective-permute-start(bf16[72,512]{1,0:T(8,128)(2,1)S(1)} %fusion), channel_id=1, source_target_pairs={{0,24},{8,16},{16,8},{24,0},{1,25},{9,17},{17,9},{25,1},{2,26},{10... | collective-permute-start | bytes 221192 | tf_op jit(solution)/shard_map/ppermute | solution.py:195
  20.3 0.0 collective-permute-done.6
  20.4 1.3 %collective-permute-start.7 = (bf16[72,512]{1,0:T(8,128)(2,1)S(1)}, bf16[72,512]{1,0:T(8,128)(2,1)S(1)}, u32[]{:S(2)}, u32[]{:S(2)}) collective-permute-start(bf16[72,512]{1,0:T(8,128)(2,1)S(1)} %fusion.1), channel_id=1, source_target_pairs={{0,24},{8,16},{16,8},{24,0},{1,25},{9,17},{17,9},{25,1},{2,26},{10... | collective-permute-start | bytes 221192 | tf_op jit(solution)/shard_map/ppermute | solution.py:195
  21.7 1.3 %collective-permute-done.5 = bf16[72,512]{1,0:T(8,128)(2,1)S(1)} collective-permute-done((bf16[72,512]{1,0:T(8,128)(2,1)S(1)}, bf16[72,512]{1,0:T(8,128)(2,1)S(1)}, u32[]{:S(2)}, u32[]{:S(2)}) %collective-permute-start.5) | collective-permute-done | bytes 73760 | tf_op jit(solution)/shard_map/ppermute | solution.py:195
  23.0 1.4 %collective-permute-done.7 = bf16[72,512]{1,0:T(8,128)(2,1)S(1)} collective-permute-done((bf16[72,512]{1,0:T(8,128)(2,1)S(1)}, bf16[72,512]{1,0:T(8,128)(2,1)S(1)}, u32[]{:S(2)}, u32[]{:S(2)}) %collective-permute-start.7) | collective-permute-done | bytes 73760 | tf_op jit(solution)/shard_map/ppermute | solution.py:195
  24.4 0.2 reshape.17
  24.6 0.7 %copy.6 = f32[12,6,2,512]{3,2,0,1:T(2,128)} copy(f32[12,6,2,512]{3,2,1,0:T(2,128)S(1)} %reshape.17) | data formatting | bytes 589824 | tf_op jit(solution)/shard_map/reshape | solution.py:223
  (7 shorter events, 0.1 us)
Async XLA Ops:
  0.0 15.8 %copy-start = (bf16[2,512,12,512]{3,1,2,0:T(8,128)(2,1)S(1)}, bf16[2,512,12,512]{3,1,2,0:T(8,128)(2,1)}, u32[]{:S(2)}) copy-start(bf16[2,512,12,512]{3,1,2,0:T(8,128)(2,1)} %param.3) | copy-start | bytes 37748740
  0.0 15.8 %copy-start.1 = (f32[512]{0:T(512)S(1)}, f32[512]{0:T(512)}, u32[]{:S(2)}) copy-start(f32[512]{0:T(512)} %param.4) | copy-start | bytes 6148
  3.7 5.1 %collective-permute-start = (bf16[48,512]{1,0:T(8,128)(2,1)S(1)}, bf16[48,512]{1,0:T(8,128)(2,1)S(1)}, u32[]{:S(2)}, u32[]{:S(2)}) collective-permute-start(bf16[48,512]{1,0:T(8,128)(2,1)S(1)} %pick.1), channel_id=1, source_target_pairs={{0,1},{1,0},{2,3},{3,2},{4,5},{5,4},{6,7},{7,6},{8,9},{9,8},{10,11... | collective-permute-start | bytes 147464 | tf_op jit(solution)/shard_map/ppermute | solution.py:195
  8.8 6.0 %collective-permute-start.3 = (bf16[48,512]{1,0:T(8,128)(2,1)S(1)}, bf16[48,512]{1,0:T(8,128)(2,1)S(1)}, u32[]{:S(2)}, u32[]{:S(2)}) collective-permute-start(bf16[48,512]{1,0:T(8,128)(2,1)S(1)} %add.38), channel_id=1, source_target_pairs={{0,6},{1,7},{2,4},{3,5},{4,2},{5,3},{6,0},{7,1},{8,14},{9,15},{10,... | collective-permute-start | bytes 147464 | tf_op jit(solution)/shard_map/ppermute | solution.py:195
  10.2 5.6 %collective-permute-start.2 = (bf16[48,512]{1,0:T(8,128)(2,1)S(1)}, bf16[48,512]{1,0:T(8,128)(2,1)S(1)}, u32[]{:S(2)}, u32[]{:S(2)}) collective-permute-start(bf16[48,512]{1,0:T(8,128)(2,1)S(1)} %add.38), channel_id=1, source_target_pairs={{0,4},{1,5},{2,6},{3,7},{4,0},{5,1},{6,2},{7,3},{8,12},{9,13},{10,... | collective-permute-start | bytes 147464 | tf_op jit(solution)/shard_map/ppermute | solution.py:195
  10.2 5.6 %collective-permute-start.1 = (bf16[48,512]{1,0:T(8,128)(2,1)S(1)}, bf16[48,512]{1,0:T(8,128)(2,1)S(1)}, u32[]{:S(2)}, u32[]{:S(2)}) collective-permute-start(bf16[48,512]{1,0:T(8,128)(2,1)S(1)} %add.38), channel_id=1, source_target_pairs={{0,2},{1,3},{2,0},{3,1},{4,6},{5,7},{6,4},{7,5},{8,10},{9,11},{10,... | collective-permute-start | bytes 147464 | tf_op jit(solution)/shard_map/ppermute | solution.py:195
  17.0 1.7 %collective-permute-start.4 = (bf16[2,72,512]{2,1,0:T(8,128)(2,1)S(1)}, bf16[2,72,512]{2,1,0:T(8,128)(2,1)S(1)}, u32[]{:S(2)}, u32[]{:S(2)}) collective-permute-start(bf16[2,72,512]{2,1,0:T(8,128)(2,1)S(1)} %get-tuple-element.11), channel_id=1, source_target_pairs={{0,8},{8,0},{16,24},{24,16},{1,9},{9,1},{17,25},{25,17},{2,10},{10... | collective-permute-start | bytes 442376 | tf_op jit(solution)/shard_map/ppermute | solution.py:195
  18.1 2.2 %collective-permute-start.6 = (bf16[2,72,512]{2,1,0:T(8,128)(2,1)S(1)}, bf16[2,72,512]{2,1,0:T(8,128)(2,1)S(1)}, u32[]{:S(2)}, u32[]{:S(2)}) collective-permute-start(bf16[2,72,512]{2,1,0:T(8,128)(2,1)S(1)} %get-tuple-element.14), channel_id=1, source_target_pairs={{0,8},{8,0},{16,24},{24,16},{1,9},{9,1},{17,25},{25,17},{2,10},{10... | collective-permute-start | bytes 442376 | tf_op jit(solution)/shard_map/ppermute | solution.py:195
  18.7 4.3 %collective-permute-start.5 = (bf16[72,512]{1,0:T(8,128)(2,1)S(1)}, bf16[72,512]{1,0:T(8,128)(2,1)S(1)}, u32[]{:S(2)}, u32[]{:S(2)}) collective-permute-start(bf16[72,512]{1,0:T(8,128)(2,1)S(1)} %fusion), channel_id=1, source_target_pairs={{0,24},{8,16},{16,8},{24,0},{1,25},{9,17},{17,9},{25,1},{2,26},{10... | collective-permute-start | bytes 221192 | tf_op jit(solution)/shard_map/ppermute | solution.py:195
  20.4 4.0 %collective-permute-start.7 = (bf16[72,512]{1,0:T(8,128)(2,1)S(1)}, bf16[72,512]{1,0:T(8,128)(2,1)S(1)}, u32[]{:S(2)}, u32[]{:S(2)}) collective-permute-start(bf16[72,512]{1,0:T(8,128)(2,1)S(1)} %fusion.1), channel_id=1, source_target_pairs={{0,24},{8,16},{16,8},{24,0},{1,25},{9,17},{17,9},{25,1},{2,26},{10... | collective-permute-start | bytes 221192 | tf_op jit(solution)/shard_map/ppermute | solution.py:195

commit v5 on v4

--- a/solution.py
+++ b/solution.py
@@ -11,7 +11,6 @@
 MIB = 2**20
 ROWS = 128
 STEPS = (6, 6)
-GROUPS = [[1], [2, 4, 6]]
 
 
 def pick_kernel(given_ref, vectors_ref, rows_ref, sites_ref, columns_ref, total_ref, given_sem, sems):
@@ -79,33 +78,6 @@
     )(source_sites, vectors)
 
 
-def load(vectors, after, start, count):
-    parts, spin_color, mode_count, site_count = vectors.shape
-
-    def load_kernel(vectors_ref, after_ref, held_ref, sems):
-        copies = [
-            pltpu.make_async_copy(vectors_ref.at[part, pl.ds(start, count)], held_ref.at[part], sems.at[part])
-            for part in range(parts)
-        ]
-        for copy in copies:
-            copy.start()
-        for copy in copies:
-            copy.wait()
-
-    shape = (parts, count, mode_count, site_count)
-    size = 2 * parts * count * mode_count * site_count
-    return pl.pallas_call(
-        load_kernel,
-        out_shape=jax.ShapeDtypeStruct(shape, vectors.dtype),
-        in_specs=[pl.BlockSpec(memory_space=pl.ANY)] * 2,
-        out_specs=pl.BlockSpec(memory_space=pltpu.VMEM),
-        scratch_shapes=[pltpu.SemaphoreType.DMA((parts,))],
-        compiler_params=pltpu.CompilerParams(vmem_limit_bytes=40 * MIB),
-        cost_estimate=pl.CostEstimate(flops=0, bytes_accessed=2 * size, transcendentals=0),
-        name="load",
-    )(vectors, after)
-
-
 def iota(shape, dim):
     return lax.broadcasted_iota(jnp.int32, shape, dim)
 
@@ -157,8 +129,7 @@
     multiply(left, vectors_ref, 0, sent_ref, kept_ref, flat_ref, 2 * columns // ways)
 
 
-def next_kernel(start, left_ref, vectors_ref, sent_ref, kept_ref, flat_ref):
-    share = 12
+def next_kernel(start, share, left_ref, vectors_ref, sent_ref, kept_ref, flat_ref):
     multiply([left_ref[0], left_ref[1]], vectors_ref, start, sent_ref, kept_ref, flat_ref, share)
 
 
@@ -186,7 +157,7 @@
     results = [first]
     start = STEPS[0]
     for count in STEPS[1:]:
-        results.append(call(functools.partial(next_kernel, start), (left, vectors), count, [], "rest"))
+        results.append(call(functools.partial(next_kernel, start, share), (left, vectors), count, [], "rest"))
         start += count
     return results
 
@@ -200,18 +171,17 @@
     vectors = jnp.transpose(eigvecs, (0, 2, 1, 3))
     parts, spin_color, mode_count, site_count = vectors.shape
     rows = pick(pltpu.with_memory_space_constraint(source_sites, pltpu.HBM), pltpu.with_memory_space_constraint(vectors, pltpu.HBM))
-    groups = list(GROUPS)
+    near = swap(rows, "sites", site_ways, 6)
+    far = [swap(rows, "sites", site_ways, bit) for bit in (5, 3)]
+    pair = rows + near
+    late = [swap(pair, "sites", site_ways, bit) for bit in (1, 2)]
+    rows = pair
+    for block in far + late:
+        rows = rows + block
     bit = 8
     while bit < site_ways:
-        groups.append([bit])
+        rows = rows + swap(rows, "sites", site_ways, bit)
         bit *= 2
-    pieces = []
-    step = spin_color // len(GROUPS)
-    for number, group in enumerate(groups):
-        if number < len(GROUPS):
-            pass
-        for block in [swap(rows, "sites", site_ways, bit) for bit in group]:
-            rows = rows + block
     halves = []
     for sent, kept in project(rows, eigenvalues, pltpu.with_memory_space_constraint(vectors, pltpu.VMEM), mode_ways):
         got = swap(sent, "modes", mode_ways, 1)

time: 25.5 us -> 26.1 us (1.024)
  the two profiles are of different devices: /device:TPU:0 before, /device:TPU:21 now
where the time goes in v5:
time: 26.1 us; the launch traced here: 26 us
  starting transfers between devices  14.9 us (57%)
  waiting for transfers between devices  6.98 us (27%)
  Pallas kernels  3.05 us (12%)
  local copies, waits for them, and re-layouts  0.91 us (3%)
    ppermute x9, starting transfers between devices, swap(): lax.ppermute(block, axis, [(index, index ^ bit) for index in range(size)])  14.9 us
    ppermute x9, waiting for transfers between devices, swap(): lax.ppermute(block, axis, [(index, index ^ bit) for index in range(size)])  6.98 us
    pallas_call x2, Pallas kernels, call(): pl.pallas_call(kernel, out_shape=[jax.ShapeDtypeStruct(shape, jnp.bfloat1...  2.18 us
    reshape x2, local copies, waits for them, and re-layouts, on_device(): total.reshape(spin_color, share, 2, site_count)  0.9 us
    pallas_call x1, Pallas kernels, pick(): pl.pallas_call(pick_kernel, out_shape=jax.ShapeDtypeStruct((rows, mode_co...  0.87 us
  transfers between devices with their start and end apart: 9, of which 6 were waited for; matrix products, arithmetic and copies ran while one was open for 0% of the time, Pallas kernels for 4%

profile of v5, /device:TPU:21, one launch (start us, length us, event | category | flops | bytes accessed | tf_op | source)
XLA Modules:
  0.0 26.0 jit_solution(15651169332336773530)
XLA Ops:
  0.0 0.0 copy-start
  0.0 0.0 copy-start.1
  0.0 0.9 %pick.1 = bf16[48,512]{1,0:T(8,128)(2,1)S(1)} custom-call(s32[2]{0:T(128)} %given_ref.1, bf16[2,12,512,512]{3,2,1,0:T(8,128)(2,1)} %bitcast.13), custom_call_target="tpu_custom_call" | custom-call | tf_op jit(solution)/shard_map/pick/pallas_call | solution.py:64
  0.9 0.2 collective-permute-start
  1.1 4.9 %collective-permute-start.2 = (bf16[48,512]{1,0:T(8,128)(2,1)S(1)}, bf16[48,512]{1,0:T(8,128)(2,1)S(1)}, u32[]{:S(2)}, u32[]{:S(2)}) collective-permute-start(bf16[48,512]{1,0:T(8,128)(2,1)S(1)} %pick.1), channel_id=1, source_target_pairs={{0,3},{1,2},{2,1},{3,0},{4,7},{5,6},{6,5},{7,4},{8,11},{9,10},{10,... | collective-permute-start | bytes 147464 | tf_op jit(solution)/shard_map/ppermute | solution.py:166
  6.0 2.0 %collective-permute-start.1 = (bf16[48,512]{1,0:T(8,128)(2,1)S(1)}, bf16[48,512]{1,0:T(8,128)(2,1)S(1)}, u32[]{:S(2)}, u32[]{:S(2)}) collective-permute-start(bf16[48,512]{1,0:T(8,128)(2,1)S(1)} %pick.1), channel_id=1, source_target_pairs={{0,5},{1,4},{2,7},{3,6},{4,1},{5,0},{6,3},{7,2},{8,13},{9,12},{10,... | collective-permute-start | bytes 147464 | tf_op jit(solution)/shard_map/ppermute | solution.py:166
  8.0 0.0 collective-permute-done
  8.1 1.8 %collective-permute-start.4 = (bf16[48,512]{1,0:T(8,128)(2,1)S(1)}, bf16[48,512]{1,0:T(8,128)(2,1)S(1)}, u32[]{:S(2)}, u32[]{:S(2)}) collective-permute-start(bf16[48,512]{1,0:T(8,128)(2,1)S(1)} %add.41), channel_id=1, source_target_pairs={{0,2},{1,3},{2,0},{3,1},{4,6},{5,7},{6,4},{7,5},{8,10},{9,11},{10,... | collective-permute-start | bytes 147464 | tf_op jit(solution)/shard_map/ppermute | solution.py:166
  9.9 1.2 %collective-permute-start.3 = (bf16[48,512]{1,0:T(8,128)(2,1)S(1)}, bf16[48,512]{1,0:T(8,128)(2,1)S(1)}, u32[]{:S(2)}, u32[]{:S(2)}) collective-permute-start(bf16[48,512]{1,0:T(8,128)(2,1)S(1)} %add.41), channel_id=1, source_target_pairs={{0,1},{1,0},{2,3},{3,2},{4,5},{5,4},{6,7},{7,6},{8,9},{9,8},{10,11... | collective-permute-start | bytes 147464 | tf_op jit(solution)/shard_map/ppermute | solution.py:166
  11.1 0.0 collective-permute-done.2
  11.1 0.2 collective-permute-done.1
  11.3 0.2 collective-permute-done.4
  11.5 1.8 %collective-permute-done.3 = bf16[48,512]{1,0:T(8,128)(2,1)S(1)} collective-permute-done((bf16[48,512]{1,0:T(8,128)(2,1)S(1)}, bf16[48,512]{1,0:T(8,128)(2,1)S(1)}, u32[]{:S(2)}, u32[]{:S(2)}) %collective-permute-start.3) | collective-permute-done | bytes 49184 | tf_op jit(solution)/shard_map/ppermute | solution.py:166
  13.3 0.0 copy-done
  13.3 0.0 copy-done.1
  13.3 1.1 %first.1 = (bf16[2,72,512]{2,1,0:T(8,128)(2,1)S(1)}, f32[2,72,512]{2,1,0:T(8,128)S(1)}, bf16[2,128,512]{2,1,0:T(8,128)(2,1)S(1)}) custom-call(bf16[48,512]{1,0:T(8,128)(2,1)S(1)} %add_add_fusion.rows_ref, f32[1,512]{1,0:T(1,128)S(1)} %bitcast.16, bf16[2,12,512,512]{3,2,1,0:T(8,128)(2,1)S(1)} %bitcast.14), custom_call_target="tpu_custom_call" | custom-call | flops 805306368 | bytes 6291456 | tf_op jit(solution)/shard_map/first/pallas_call | solution.py:144
  14.4 3.4 %collective-permute-start.5 = (bf16[2,72,512]{2,1,0:T(8,128)(2,1)S(1)}, bf16[2,72,512]{2,1,0:T(8,128)(2,1)S(1)}, u32[]{:S(2)}, u32[]{:S(2)}) collective-permute-start(bf16[2,72,512]{2,1,0:T(8,128)(2,1)S(1)} %get-tuple-element.11), channel_id=1, source_target_pairs={{0,8},{8,0},{16,24},{24,16},{1,9},{9,1},{17,25},{25,17},{2,10},{10... | collective-permute-start | bytes 442376 | tf_op jit(solution)/shard_map/ppermute | solution.py:166
  17.8 1.0 %rest.1 = (bf16[2,72,512]{2,1,0:T(8,128)(2,1)S(1)}, f32[2,72,512]{2,1,0:T(8,128)S(1)}) custom-call(bf16[2,128,512]{2,1,0:T(8,128)(2,1)S(1)} %get-tuple-element.12.left_ref, bf16[2,12,512,512]{3,2,1,0:T(8,128)(2,1)S(1)} %bitcast.15), custom_call_target="tpu_custom_call" | custom-call | flops 805306368 | bytes 6291456 | tf_op jit(solution)/shard_map/rest/pallas_call | solution.py:144
  18.8 0.1 collective-permute-start.7
  18.9 0.0 collective-permute-done.5
  19.0 0.7 %collective-permute-start.6 = (bf16[72,512]{1,0:T(8,128)(2,1)S(1)}, bf16[72,512]{1,0:T(8,128)(2,1)S(1)}, u32[]{:S(2)}, u32[]{:S(2)}) collective-permute-start(bf16[72,512]{1,0:T(8,128)(2,1)S(1)} %fusion), channel_id=1, source_target_pairs={{0,24},{8,16},{16,8},{24,0},{1,25},{9,17},{17,9},{25,1},{2,26},{10... | collective-permute-start | bytes 221192 | tf_op jit(solution)/shard_map/ppermute | solution.py:166
  19.6 0.7 %collective-permute-done.7 = bf16[2,72,512]{2,1,0:T(8,128)(2,1)S(1)} collective-permute-done((bf16[2,72,512]{2,1,0:T(8,128)(2,1)S(1)}, bf16[2,72,512]{2,1,0:T(8,128)(2,1)S(1)}, u32[]{:S(2)}, u32[]{:S(2)}) %collective-permute-start.7) | collective-permute-done | bytes 147488 | tf_op jit(solution)/shard_map/ppermute | solution.py:166
  20.3 0.6 %collective-permute-start.8 = (bf16[72,512]{1,0:T(8,128)(2,1)S(1)}, bf16[72,512]{1,0:T(8,128)(2,1)S(1)}, u32[]{:S(2)}, u32[]{:S(2)}) collective-permute-start(bf16[72,512]{1,0:T(8,128)(2,1)S(1)} %fusion.1), channel_id=1, source_target_pairs={{0,24},{8,16},{16,8},{24,0},{1,25},{9,17},{17,9},{25,1},{2,26},{10... | collective-permute-start | bytes 221192 | tf_op jit(solution)/shard_map/ppermute | solution.py:166
  20.9 3.0 %collective-permute-done.6 = bf16[72,512]{1,0:T(8,128)(2,1)S(1)} collective-permute-done((bf16[72,512]{1,0:T(8,128)(2,1)S(1)}, bf16[72,512]{1,0:T(8,128)(2,1)S(1)}, u32[]{:S(2)}, u32[]{:S(2)}) %collective-permute-start.6) | collective-permute-done | bytes 73760 | tf_op jit(solution)/shard_map/ppermute | solution.py:166
  23.9 1.1 %collective-permute-done.8 = bf16[72,512]{1,0:T(8,128)(2,1)S(1)} collective-permute-done((bf16[72,512]{1,0:T(8,128)(2,1)S(1)}, bf16[72,512]{1,0:T(8,128)(2,1)S(1)}, u32[]{:S(2)}, u32[]{:S(2)}) %collective-permute-start.8) | collective-permute-done | bytes 73760 | tf_op jit(solution)/shard_map/ppermute | solution.py:166
  25.1 0.2 reshape.17
  25.3 0.7 %copy.6 = f32[12,6,2,512]{3,2,0,1:T(2,128)} copy(f32[12,6,2,512]{3,2,1,0:T(2,128)S(1)} %reshape.17) | data formatting | bytes 589824 | tf_op jit(solution)/shard_map/reshape | solution.py:193
  (7 shorter events, 0.1 us)
Async XLA Ops:
  0.0 13.3 %copy-start = (bf16[2,512,12,512]{3,1,2,0:T(8,128)(2,1)S(1)}, bf16[2,512,12,512]{3,1,2,0:T(8,128)(2,1)}, u32[]{:S(2)}) copy-start(bf16[2,512,12,512]{3,1,2,0:T(8,128)(2,1)} %param.3) | copy-start | bytes 37748740
  0.0 13.3 %copy-start.1 = (f32[512]{0:T(512)S(1)}, f32[512]{0:T(512)}, u32[]{:S(2)}) copy-start(f32[512]{0:T(512)} %param.4) | copy-start | bytes 6148
  0.9 7.2 %collective-permute-start = (bf16[48,512]{1,0:T(8,128)(2,1)S(1)}, bf16[48,512]{1,0:T(8,128)(2,1)S(1)}, u32[]{:S(2)}, u32[]{:S(2)}) collective-permute-start(bf16[48,512]{1,0:T(8,128)(2,1)S(1)} %pick.1), channel_id=1, source_target_pairs={{0,6},{1,7},{2,4},{3,5},{4,2},{5,3},{6,0},{7,1},{8,14},{9,15},{10,... | collective-permute-start | bytes 147464 | tf_op jit(solution)/shard_map/ppermute | solution.py:166
  1.1 10.0 %collective-permute-start.2 = (bf16[48,512]{1,0:T(8,128)(2,1)S(1)}, bf16[48,512]{1,0:T(8,128)(2,1)S(1)}, u32[]{:S(2)}, u32[]{:S(2)}) collective-permute-start(bf16[48,512]{1,0:T(8,128)(2,1)S(1)} %pick.1), channel_id=1, source_target_pairs={{0,3},{1,2},{2,1},{3,0},{4,7},{5,6},{6,5},{7,4},{8,11},{9,10},{10,... | collective-permute-start | bytes 147464 | tf_op jit(solution)/shard_map/ppermute | solution.py:166
  6.0 5.3 %collective-permute-start.1 = (bf16[48,512]{1,0:T(8,128)(2,1)S(1)}, bf16[48,512]{1,0:T(8,128)(2,1)S(1)}, u32[]{:S(2)}, u32[]{:S(2)}) collective-permute-start(bf16[48,512]{1,0:T(8,128)(2,1)S(1)} %pick.1), channel_id=1, source_target_pairs={{0,5},{1,4},{2,7},{3,6},{4,1},{5,0},{6,3},{7,2},{8,13},{9,12},{10,... | collective-permute-start | bytes 147464 | tf_op jit(solution)/shard_map/ppermute | solution.py:166
  8.1 3.4 %collective-permute-start.4 = (bf16[48,512]{1,0:T(8,128)(2,1)S(1)}, bf16[48,512]{1,0:T(8,128)(2,1)S(1)}, u32[]{:S(2)}, u32[]{:S(2)}) collective-permute-start(bf16[48,512]{1,0:T(8,128)(2,1)S(1)} %add.41), channel_id=1, source_target_pairs={{0,2},{1,3},{2,0},{3,1},{4,6},{5,7},{6,4},{7,5},{8,10},{9,11},{10,... | collective-permute-start | bytes 147464 | tf_op jit(solution)/shard_map/ppermute | solution.py:166
  9.9 3.4 %collective-permute-start.3 = (bf16[48,512]{1,0:T(8,128)(2,1)S(1)}, bf16[48,512]{1,0:T(8,128)(2,1)S(1)}, u32[]{:S(2)}, u32[]{:S(2)}) collective-permute-start(bf16[48,512]{1,0:T(8,128)(2,1)S(1)} %add.41), channel_id=1, source_target_pairs={{0,1},{1,0},{2,3},{3,2},{4,5},{5,4},{6,7},{7,6},{8,9},{9,8},{10,11... | collective-permute-start | bytes 147464 | tf_op jit(solution)/shard_map/ppermute | solution.py:166
  14.4 4.5 %collective-permute-start.5 = (bf16[2,72,512]{2,1,0:T(8,128)(2,1)S(1)}, bf16[2,72,512]{2,1,0:T(8,128)(2,1)S(1)}, u32[]{:S(2)}, u32[]{:S(2)}) collective-permute-start(bf16[2,72,512]{2,1,0:T(8,128)(2,1)S(1)} %get-tuple-element.11), channel_id=1, source_target_pairs={{0,8},{8,0},{16,24},{24,16},{1,9},{9,1},{17,25},{25,17},{2,10},{10... | collective-permute-start | bytes 442376 | tf_op jit(solution)/shard_map/ppermute | solution.py:166
  18.8 1.4 %collective-permute-start.7 = (bf16[2,72,512]{2,1,0:T(8,128)(2,1)S(1)}, bf16[2,72,512]{2,1,0:T(8,128)(2,1)S(1)}, u32[]{:S(2)}, u32[]{:S(2)}) collective-permute-start(bf16[2,72,512]{2,1,0:T(8,128)(2,1)S(1)} %get-tuple-element.14), channel_id=1, source_target_pairs={{0,8},{8,0},{16,24},{24,16},{1,9},{9,1},{17,25},{25,17},{2,10},{10... | collective-permute-start | bytes 442376 | tf_op jit(solution)/shard_map/ppermute | solution.py:166
  19.0 4.9 %collective-permute-start.6 = (bf16[72,512]{1,0:T(8,128)(2,1)S(1)}, bf16[72,512]{1,0:T(8,128)(2,1)S(1)}, u32[]{:S(2)}, u32[]{:S(2)}) collective-permute-start(bf16[72,512]{1,0:T(8,128)(2,1)S(1)} %fusion), channel_id=1, source_target_pairs={{0,24},{8,16},{16,8},{24,0},{1,25},{9,17},{17,9},{25,1},{2,26},{10... | collective-permute-start | bytes 221192 | tf_op jit(solution)/shard_map/ppermute | solution.py:166
  20.3 4.8 %collective-permute-start.8 = (bf16[72,512]{1,0:T(8,128)(2,1)S(1)}, bf16[72,512]{1,0:T(8,128)(2,1)S(1)}, u32[]{:S(2)}, u32[]{:S(2)}) collective-permute-start(bf16[72,512]{1,0:T(8,128)(2,1)S(1)} %fusion.1), channel_id=1, source_target_pairs={{0,24},{8,16},{16,8},{24,0},{1,25},{9,17},{17,9},{25,1},{2,26},{10... | collective-permute-start | bytes 221192 | tf_op jit(solution)/shard_map/ppermute | solution.py:166
